TPU v7x, 512 devices: a whole 4x4x16 slice. The times are simulated.
512 devices in a mesh: ctx: 64 (over x, z), tp: 8 (over y, core).
Axes of the slice: x: 4, y: 4, z: 16, core: 2. Of those that a mesh axis runs over, the one named last changes fastest.
Arguments:
- gate_in: bfloat16 [8192, 4096], P('ctx', 'tp'), may hold values from -6 to 6
- value_in: bfloat16 [8192, 4096], P('ctx', 'tp'), may hold values from -6 to 6
- gate_out: bfloat16 [8192, 4096], P('ctx', 'tp'), may hold values from -6 to 6
- filters: bfloat16 [8192, 4096], P('ctx', 'tp'), may hold values from -1.1 to 1.1, as said below
- skip_gain: float32 [4096], P('tp'), may hold values from -4 to 4
- out_weight: bfloat16 [4096, 4096], P('ctx', 'tp'), may hold values from -0.09375 to 0.09375
Outputs:
- mixed: bfloat16 [8192, 4096], P('ctx', 'tp')
Inputs may be any that keep to these rules, and one draw needn't show every extreme that they name: `filters`: one filter a channel over 8192 lags.
All inputs are finite; a program needn't handle non-finite values.
Results may differ from a plain program's by a relative error of at most 0.013.
Values may be sent and summed in bfloat16 or wider, within the bound.
No kernel may reach another device: no remote copies, remote signals or barrier semaphores. Data moves between devices by JAX's collectives and lax.ppermute only.
A program may use at most 64 MiB of HBM per device.

v0:
```python
import math

import jax
import jax.numpy as jnp
from jax import lax
from jax.sharding import PartitionSpec as P


def angle_tables(count_rows, count_cols, period):
    index_prod = (
        jnp.arange(count_rows, dtype=jnp.int32)[:, None]
        * jnp.arange(count_cols, dtype=jnp.int32)[None, :]
        % period
    )
    angles = index_prod.astype(jnp.float32) * (2.0 * math.pi / period)
    return (jnp.cos(angles), jnp.sin(angles))


def einsum_high(form, left, right):
    return jnp.einsum(form, left, right, precision=lax.Precision.HIGHEST)


def dft_rows(real, imag, sign):
    count = real.shape[-2]
    first = 1 << (count.bit_length() - 1) // 2
    while count % first:
        first = first // 2
    second = count // first
    shape_in = real.shape[:-2] + (first, second, real.shape[-1])
    part_re = real.reshape(shape_in)
    part_im = imag.reshape(shape_in)
    cos_a, sin_a = angle_tables(first, first, first)
    section_re = einsum_high("...abf,as->...sbf", part_re, cos_a) - sign * einsum_high(
        "...abf,as->...sbf", part_im, sin_a
    )
    section_im = einsum_high("...abf,as->...sbf", part_im, cos_a) + sign * einsum_high(
        "...abf,as->...sbf", part_re, sin_a
    )
    twist_idx = (
        jnp.arange(first, dtype=jnp.int32)[:, None]
        * jnp.arange(second, dtype=jnp.int32)[None, :]
        % count
    )
    twist_ang = twist_idx.astype(jnp.float32) * (2.0 * math.pi / count)
    twist_cos = jnp.cos(twist_ang)[:, :, None]
    twist_sin = sign * jnp.sin(twist_ang)[:, :, None]
    turn_re = section_re * twist_cos - section_im * twist_sin
    turn_im = section_re * twist_sin + section_im * twist_cos
    cos_b, sin_b = angle_tables(second, second, second)
    out_re = einsum_high("...sbf,bt->...stf", turn_re, cos_b) - sign * einsum_high(
        "...sbf,bt->...stf", turn_im, sin_b
    )
    out_im = einsum_high("...sbf,bt->...stf", turn_im, cos_b) + sign * einsum_high(
        "...sbf,bt->...stf", turn_re, sin_b
    )
    out_re = jnp.swapaxes(out_re, -3, -2).reshape(real.shape)
    out_im = jnp.swapaxes(out_im, -3, -2).reshape(real.shape)
    return (out_re, out_im)


def move_rows(values):
    return lax.all_to_all(values, "ctx", split_axis=1, concat_axis=2, tiled=True)


def spread_conv(signal, filters):
    members = lax.axis_size("ctx")
    my_index = lax.axis_index("ctx")
    seq_rows, channels = signal.shape
    block_rows = seq_rows // members
    span_k = 2 * members
    total_len = span_k * seq_rows
    stacked = jnp.stack([signal, filters])[:, :, None, :]
    received = move_rows(stacked).astype(jnp.float32)
    cos_c, sin_c = angle_tables(members, span_k, span_k)
    first_re = einsum_high("grcf,ck->gkrf", received, cos_c)
    first_im = -einsum_high("grcf,ck->gkrf", received, sin_c)
    local_pos = my_index * block_rows + jnp.arange(block_rows, dtype=jnp.int32)
    twist_idx = jnp.arange(span_k, dtype=jnp.int32)[:, None] * local_pos[None, :] % total_len
    twist_ang = twist_idx.astype(jnp.float32) * (2.0 * math.pi / total_len)
    twist_cos = jnp.cos(twist_ang)[None, :, :, None]
    twist_sin = -jnp.sin(twist_ang)[None, :, :, None]
    turned_re = first_re * twist_cos - first_im * twist_sin
    turned_im = first_re * twist_sin + first_im * twist_cos
    spectrum = jnp.concatenate([turned_re, turned_im], 0)
    owned = lax.all_to_all(spectrum, "ctx", split_axis=1, concat_axis=2, tiled=True)
    part_re = owned[0:2]
    part_im = owned[2:4]
    freq_re, freq_im = dft_rows(part_re, part_im, -1.0)
    prod_re = freq_re[0] * freq_re[1] - freq_im[0] * freq_im[1]
    prod_im = freq_re[0] * freq_im[1] + freq_im[0] * freq_re[1]
    back_re, back_im = dft_rows(prod_re, prod_im, 1.0)
    own_freq = 2 * my_index + jnp.arange(2, dtype=jnp.int32)
    undo_idx = own_freq[:, None] * jnp.arange(seq_rows, dtype=jnp.int32)[None, :] % total_len
    undo_ang = undo_idx.astype(jnp.float32) * (2.0 * math.pi / total_len)
    undo_cos = jnp.cos(undo_ang)[:, :, None]
    undo_sin = jnp.sin(undo_ang)[:, :, None]
    level_re = back_re * undo_cos - back_im * undo_sin
    level_im = back_re * undo_sin + back_im * undo_cos
    returned = lax.all_to_all(
        jnp.stack([level_re, level_im]), "ctx", split_axis=2, concat_axis=1, tiled=True
    )
    positions = (
        einsum_high("krf,ck->crf", returned[0], cos_c)
        - einsum_high("krf,ck->crf", returned[1], sin_c)
    ) / total_len
    result = move_rows(positions.astype(jnp.bfloat16)[None])
    return result[0, 0]


def per_device(gate_in, value_in, gate_out, filters, skip_gain, out_weight):
    signal = (gate_in.astype(jnp.float32) * value_in.astype(jnp.float32)).astype(jnp.bfloat16)
    conv = spread_conv(signal, filters)
    gated = (
        gate_out.astype(jnp.float32)
        * (conv.astype(jnp.float32) + skip_gain[None, :] * signal.astype(jnp.float32))
    ).astype(jnp.bfloat16)
    whole = lax.all_gather(gated, "tp", axis=1, tiled=True)
    mixed = jnp.dot(
        whole,
        lax.all_gather(out_weight, "ctx", axis=0, tiled=True),
        preferred_element_type=jnp.float32,
    )
    return mixed.astype(jnp.bfloat16)


def solution(mesh):
    placed = (
        P("ctx", "tp"),
        P("ctx", "tp"),
        P("ctx", "tp"),
        P("ctx", "tp"),
        P("tp"),
        P("ctx", "tp"),
    )
    return jax.shard_map(
        per_device, mesh=mesh, in_specs=placed, out_specs=P("ctx", "tp"), check_vma=False
    )
```

profile of v0, /device:TPU:1, one launch (start us, length us, event | category | flops | bytes accessed | tf_op | source)
XLA Modules:
  0.0 321.0 jit_solution(12289791233125148895)
XLA Ops:
  6.5 1.0 fusion.42
  7.5 0.9 maximum_bitcast_fusion
  8.5 1.0 copy.42
  9.4 19.1 %all-to-all-start = ((bf16[2,128,1,512]{3,0,2,1:T(2,128)(2,1)}), bf16[2,128,1,512]{3,0,2,1:T(2,128)(2,1)S(1)}, u32[]{:S(2)}, u32[]{:S(2)}) async-start(bf16[2,128,1,512]{3,0,2,1:T(2,128)(2,1)} %copy.42), calls=%async_computation | async-start | bytes 524288 | tf_op jit(solution)/shard_map/all_to_all | solution.py:62
  28.7 18.9 %all-to-all-done = bf16[2,128,1,512]{3,0,2,1:T(2,128)(2,1)S(1)} async-done(((bf16[2,128,1,512]{3,0,2,1:T(2,128)(2,1)}), bf16[2,128,1,512]{3,0,2,1:T(2,128)(2,1)S(1)}, u32[]{:S(2)}, u32[]{:S(2)}) %all-to-all-start) | async-done | bytes 262176 | tf_op jit(solution)/shard_map/all_to_all | solution.py:62
  48.4 1.0 subtract_bitcast_fusion.1
  49.5 3.0 copy.44
  52.5 7.6 %all-to-all-start.1 = ((f32[4,128,2,512]{3,2,0,1:T(2,128)}), f32[4,128,2,512]{3,2,0,1:T(2,128)S(1)}, u32[]{:S(2)}, u32[]{:S(2)}) async-start(f32[4,128,2,512]{3,2,0,1:T(2,128)} %copy.44), calls=%async_computation.1 | async-start | bytes 4194304 | tf_op jit(solution)/shard_map/all_to_all | solution.py:85
  61.6 95.3 %all-to-all-done.1 = f32[4,128,2,512]{3,2,0,1:T(2,128)S(1)} async-done(((f32[4,128,2,512]{3,2,0,1:T(2,128)}), f32[4,128,2,512]{3,2,0,1:T(2,128)S(1)}, u32[]{:S(2)}, u32[]{:S(2)}) %all-to-all-start.1) | async-done | bytes 2097184 | tf_op jit(solution)/shard_map/all_to_all | solution.py:85
  156.9 1.6 copy.132
  158.5 0.8 fusion.205
  159.3 1.5 fusion.17
  160.8 1.5 fusion.21
  162.4 1.6 fusion.4
  163.9 1.8 subtract_bitcast_fusion
  165.8 1.5 fusion.15
  167.3 1.7 fusion.11
  169.0 1.5 fusion.3
  170.5 1.6 fusion.1
  173.0 0.8 fusion.31
  173.8 0.8 fusion.35
  174.6 0.8 convolution_add_fusion.1
  175.5 0.9 subtract_bitcast_fusion.2
  176.4 0.8 fusion.29
  177.3 0.8 fusion.25
  178.1 0.9 fusion.7
  179.0 0.9 fusion.6
  180.6 1.0 copy.66
  181.6 76.4 %all_to_all.57 = f32[2,2,128,512]{3,1,0,2:T(2,128)S(1)} all-to-all(f32[2,2,128,512]{3,1,0,2:T(2,128)S(1)} %copy.66), channel_id=1, replica_groups=mesh['ctx'=64,'tp'=8] {'ctx'}, dimensions={2} | all-to-all | bytes 2097152 | tf_op jit(solution)/shard_map/all_to_all | solution.py:99
  260.9 22.2 %all_to_all.58 = bf16[1,64,2,512]{3,2,0,1:T(2,128)(2,1)S(1)} all-to-all(bf16[1,64,2,512]{3,2,0,1:T(2,128)(2,1)S(1)} %copy.70), channel_id=1, replica_groups=mesh['ctx'=64,'tp'=8] {'ctx'}, dimensions={1} | all-to-all | bytes 262144 | tf_op jit(solution)/shard_map/all_to_all | solution.py:62
  283.9 26.1 %all-gather.3.cloned.1.call-done = bf16[128,4096]{1,0:T(8,128)(2,1)} async-done(((bf16[128,512]{1,0:T(8,128)(2,1)}), bf16[128,4096]{1,0:T(8,128)(2,1)}) %all-gather.3.cloned.1.call-update) | async-done | bytes 1048592 | tf_op jit(solution)/shard_map/all_gather | solution.py:117
  310.1 3.9 %convolution_convert_fusion = bf16[128,512]{1,0:T(8,128)(2,1)} fusion(bf16[128,4096]{1,0:T(8,128)(2,1)} %all-gather.3.cloned.1.call-done, bf16[4096,512]{1,0:T(8,128)(2,1)} %all-gather.5.cloned.1.call-done), kind=kOutput, calls=%fused_computation.22 | convolution fusion | flops 536936448 | bytes 5373952 | tf_op jit(solution)/shard_map/dot_general | solution.py:118
  (36 shorter events, 7.6 us)
Async XLA Ops:
  9.4 38.2 %all-to-all-start = ((bf16[2,128,1,512]{3,0,2,1:T(2,128)(2,1)}), bf16[2,128,1,512]{3,0,2,1:T(2,128)(2,1)S(1)}, u32[]{:S(2)}, u32[]{:S(2)}) async-start(bf16[2,128,1,512]{3,0,2,1:T(2,128)(2,1)} %copy.42), calls=%async_computation | async-start | bytes 524288 | tf_op jit(solution)/shard_map/all_to_all | solution.py:62
  52.5 104.4 %all-to-all-start.1 = ((f32[4,128,2,512]{3,2,0,1:T(2,128)}), f32[4,128,2,512]{3,2,0,1:T(2,128)S(1)}, u32[]{:S(2)}, u32[]{:S(2)}) async-start(f32[4,128,2,512]{3,2,0,1:T(2,128)} %copy.44), calls=%async_computation.1 | async-start | bytes 4194304 | tf_op jit(solution)/shard_map/all_to_all | solution.py:85
  60.1 223.8 %all-gather.5.cloned.1.call-start = ((), (), s32[]{:S(2)}) async-start(), calls=%async_computation.5 | async-start | bytes 4259840 | tf_op jit(solution)/shard_map/all_gather | solution.py:120
  60.8 249.2 %all-gather.3.cloned.1.call-start = ((), (), s32[]{:S(2)}) async-start(), calls=%async_computation.4 | async-start | bytes 1179648 | tf_op jit(solution)/shard_map/all_gather | solution.py:117
  259.2 23.9 %copy-start = (bf16[128,512]{1,0:T(8,128)(2,1)S(1)}, bf16[128,512]{1,0:T(8,128)(2,1)}, u32[]{:S(2)}) copy-start(bf16[128,512]{1,0:T(8,128)(2,1)} %param.7) | copy-start | bytes 393220
  259.2 23.9 %copy-start.1 = (bf16[128,512]{1,0:T(8,128)(2,1)S(1)}, bf16[128,512]{1,0:T(8,128)(2,1)}, u32[]{:S(2)}) copy-start(bf16[128,512]{1,0:T(8,128)(2,1)} %param.6) | copy-start | bytes 393220
  259.2 23.9 %copy-start.2 = (bf16[128,512]{1,0:T(8,128)(2,1)S(1)}, bf16[128,512]{1,0:T(8,128)(2,1)}, u32[]{:S(2)}) copy-start(bf16[128,512]{1,0:T(8,128)(2,1)} %param.8) | copy-start | bytes 393220
  259.2 23.9 %copy-start.3 = (f32[512]{0:T(512)S(1)}, f32[512]{0:T(512)}, u32[]{:S(2)}) copy-start(f32[512]{0:T(512)} %param.10) | copy-start | bytes 6148
Sparse Core Ops, SparseCore 0:
  63.9 191.4 all-gather.4
  284.0 26.0 all-gather.2
where the time goes:
time: 326 us; the launch traced here: 321 us
  waiting for transfers between devices  141 us (43%)
  blocking collectives  98.6 us (30%)
  starting transfers between devices  27.2 us (8%)
  matrix products  26.2 us (8%)
  between operations  14 us (4%)
  local copies, waits for them, and re-layouts  9.75 us (3%)
  other arithmetic  4.13 us (1%)
    all_to_all x1, waiting for transfers between devices, spread_conv(): lax.all_to_all(spectrum, 'ctx', split_axis=1, concat_axis=2, tiled=True)  95.3 us
    all_to_all x1, blocking collectives, spread_conv(): lax.all_to_all(jnp.stack([level_re, level_im]), 'ctx', split_axis=2, conc...  76.4 us
    all_gather x1, waiting for transfers between devices, per_device(): whole = lax.all_gather(gated, 'tp', axis=1, tiled=True)  26.1 us
    dot_general x20, matrix products, einsum_high(): return jnp.einsum(form, left, right, precision=lax.Precision.HIGHEST)  22.3 us
    all_to_all x1, blocking collectives, move_rows(): lax.all_to_all(values, 'ctx', split_axis=1, concat_axis=2, tiled=True)  22.2 us
    all_to_all x1, starting transfers between devices, move_rows(): lax.all_to_all(values, 'ctx', split_axis=1, concat_axis=2, tiled=True)  19.1 us
    all_to_all x1, waiting for transfers between devices, move_rows(): lax.all_to_all(values, 'ctx', split_axis=1, concat_axis=2, tiled=True)  18.9 us
    all_to_all x1, starting transfers between devices, spread_conv(): lax.all_to_all(spectrum, 'ctx', split_axis=1, concat_axis=2, tiled=True)  7.59 us
  transfers between devices with their start and end apart: 4, of which 3 were waited for; matrix products, arithmetic and copies ran while one was open for 9% of the time, Pallas kernels for 0%

commit v1 on v0

v1 whole, which is shorter than its diff:
```python
import math

import jax
import jax.numpy as jnp
import numpy as np
from jax import lax
from jax.experimental import pallas as pl
from jax.experimental.pallas import tpu as pltpu
from jax.sharding import Mesh
from jax.sharding import PartitionSpec as P

F32 = jnp.float32
BF16 = jnp.bfloat16
SEQ = 8192
BLOCK = 128
NBLK = SEQ // BLOCK
VMEM_LIMIT = 40 * 1024 * 1024


def split_table(values):
    values = np.asarray(values, np.float64)
    high = values.astype(np.float32).astype(BF16)
    low = (values - high.astype(np.float64)).astype(np.float32).astype(BF16)
    return high, low


def tables():
    n1 = np.arange(NBLK)
    k1 = np.arange(NBLK) + 0.25
    n2 = np.arange(BLOCK)
    ang = 2.0 * math.pi / NBLK * (k1[:, None] * n1[None, :])
    first = np.concatenate([np.cos(ang), -np.sin(ang)], 0)
    first = np.concatenate(split_table(first), 1)
    tw = 2.0 * math.pi / SEQ * (k1[:, None] * n2[None, :])
    twist = np.stack([np.cos(tw), -np.sin(tw)]).astype(np.float32)
    th = 2.0 * math.pi / BLOCK * ((n2[:, None] * n2[None, :]) % BLOCK)
    c, s = np.cos(th), np.sin(th)
    fwd = np.block([[c, -s], [s, c]])
    second = np.stack(split_table(fwd) + split_table(fwd.T))
    last = np.concatenate([np.cos(ang.T), -np.sin(ang.T)], 1) / SEQ
    high, low = split_table(last)
    last = np.concatenate([high, high, low], 1)
    return first, twist, second, last


def split(x):
    high = x.astype(BF16)
    return high, (x - high.astype(F32)).astype(BF16)


def mm(a, b):
    return jnp.dot(a, b, preferred_element_type=F32)


def pack_kernel(gi_ref, vi_ref, f_ref, out_ref):
    signal = (gi_ref[...].astype(F32) * vi_ref[...].astype(F32)).astype(BF16)
    sig_t = signal.astype(F32).T.reshape(NBLK, 8, BLOCK)
    fil_t = f_ref[...].astype(F32).T.reshape(NBLK, 8, BLOCK)
    out_ref[...] = jnp.concatenate([sig_t, fil_t], 1).astype(BF16)


def conv_kernel(r_ref, first_ref, twist_ref, second_ref, last_ref, out_ref, xs, xx, hi, lo, spec, dd, ys):
    xs[...] = r_ref[...].astype(F32)
    for c in range(8):
        for part in range(2):
            x = xs[:, 8 * part + c, :].astype(BF16)
            at = pl.ds((2 * c + part) * BLOCK, BLOCK)
            xx[0:NBLK, at] = x
            xx[NBLK:, at] = x
    tre, tim = twist_ref[0], twist_ref[1]
    for j in range(16):
        a = mm(first_ref[...], xx[:, j * BLOCK : (j + 1) * BLOCK])
        re, im = a[:NBLK], a[NBLK:]
        turned = jnp.concatenate([re * tre - im * tim, re * tim + im * tre], 1)
        rows = pl.ds(j * NBLK, NBLK)
        hi[rows, :], lo[rows, :] = split(turned)
    spec[...] = mm(hi[...], second_ref[0]) + mm(lo[...], second_ref[0]) + mm(hi[...], second_ref[1])
    for c in range(8):
        s = spec[pl.ds(2 * c * NBLK, NBLK), :]
        f = spec[pl.ds((2 * c + 1) * NBLK, NBLK), :]
        sr, si, fr, fi = s[:, :BLOCK], s[:, BLOCK:], f[:, :BLOCK], f[:, BLOCK:]
        rows = pl.ds(c * NBLK, NBLK)
        hi[rows, :], lo[rows, :] = split(jnp.concatenate([sr * fr - si * fi, sr * fi + si * fr], 1))
    half = pl.ds(0, 8 * NBLK)
    spec[half, :] = (
        mm(hi[half, :], second_ref[2]) + mm(lo[half, :], second_ref[2]) + mm(hi[half, :], second_ref[3])
    )
    for c in range(8):
        b = spec[pl.ds(c * NBLK, NBLK), :]
        br, bi = b[:, :BLOCK], b[:, BLOCK:]
        d_hi, d_lo = split(jnp.concatenate([br * tre + bi * tim, bi * tre - br * tim], 0))
        at = pl.ds(c * BLOCK, BLOCK)
        dd[0:128, at] = d_hi
        dd[128:256, at] = d_lo
        dd[256:384, at] = d_hi
    y = mm(last_ref[...], dd[...])
    for c in range(8):
        ys[:, c, :] = y[:, c * BLOCK : (c + 1) * BLOCK]
    out_ref[...] = ys[...].astype(BF16)


def gate_kernel(r_ref, gi_ref, vi_ref, go_ref, skip_ref, out_ref):
    conv = r_ref[...].astype(F32).reshape(8 * NBLK, BLOCK).T
    signal = (gi_ref[...].astype(F32) * vi_ref[...].astype(F32)).astype(BF16).astype(F32)
    out_ref[...] = (go_ref[...].astype(F32) * (conv + skip_ref[...] * signal)).astype(BF16)


def project_kernel(core_ref, g_ref, w_ref, out_ref):
    total = jnp.zeros(out_ref.shape, F32)
    for y in range(4):
        total += mm(g_ref[y], w_ref[:, y].reshape(512, 512))
    out_ref[...] = total


def project_end_kernel(core_ref, g_ref, w_ref, p_ref, out_ref):
    total = p_ref[...]
    for y in range(4):
        total += mm(g_ref[y], w_ref[:, y].reshape(512, 512))
    out_ref[...] = total.astype(BF16)


PARAMS = pltpu.CompilerParams(vmem_limit_bytes=VMEM_LIMIT)


def shape(dims, kind=BF16):
    return jax.ShapeDtypeStruct(dims, kind)


def project(core, gathered, weight, partial=None):
    ins = [
        pl.BlockSpec((4, BLOCK, 512), lambda i, c: (0, 0, 0)),
        pl.BlockSpec((8, 4, 64, 512), lambda i, c: (c[0], 0, 0, 0)),
    ]
    args = [gathered, weight]
    body, kind = project_kernel, F32
    if partial is not None:
        ins.append(pl.BlockSpec((BLOCK, 512), lambda i, c: (0, 0)))
        args.append(partial)
        body, kind = project_end_kernel, BF16
    return pl.pallas_call(
        body,
        grid_spec=pltpu.PrefetchScalarGridSpec(
            num_scalar_prefetch=1,
            grid=(1,),
            in_specs=ins,
            out_specs=pl.BlockSpec((BLOCK, 512), lambda i, c: (0, 0)),
        ),
        out_shape=shape((BLOCK, 512), kind),
        compiler_params=PARAMS,
    )(core, *args)


def per_device(gate_in, value_in, gate_out, filters, skip_gain, out_weight):
    first, twist, second, last = tables()
    packed = pl.pallas_call(
        pack_kernel, out_shape=shape((NBLK, 16, BLOCK)), compiler_params=PARAMS
    )(gate_in, value_in, filters)
    near = lax.all_gather(out_weight, "x", axis=0)
    packed, near = lax.optimization_barrier((packed, near))
    weight = lax.all_gather(near, "z", axis=0)
    moved = lax.all_to_all(packed, ("x", "z"), split_axis=0, concat_axis=0, tiled=True)
    conv = pl.pallas_call(
        conv_kernel,
        out_shape=shape((NBLK, 8, BLOCK)),
        scratch_shapes=[
            pltpu.VMEM((NBLK, 16, BLOCK), F32),
            pltpu.VMEM((128, 16 * BLOCK), BF16),
            pltpu.VMEM((16 * NBLK, 256), BF16),
            pltpu.VMEM((16 * NBLK, 256), BF16),
            pltpu.VMEM((16 * NBLK, 256), F32),
            pltpu.VMEM((384, 8 * BLOCK), BF16),
            pltpu.VMEM((NBLK, 8, BLOCK), F32),
        ],
        compiler_params=PARAMS,
    )(moved, first, twist, second, last)
    back = lax.all_to_all(conv, ("x", "z"), split_axis=0, concat_axis=0, tiled=True)
    gated = pl.pallas_call(
        gate_kernel, out_shape=shape((BLOCK, 512)), compiler_params=PARAMS
    )(back, gate_in, value_in, gate_out, skip_gain[None, :])
    mine = lax.all_gather(gated, "y", axis=0)
    other = lax.ppermute(mine, "core", [(0, 1), (1, 0)])
    core = lax.axis_index("core").astype(jnp.int32)[None]
    partial = project(core, mine, weight)
    return project(1 - core, other, weight, partial)


def solution(mesh):
    fine = Mesh(mesh.devices.reshape(4, 16, 4, 2), ("x", "z", "y", "core"))
    rows, cols = ("x", "z"), ("y", "core")
    whole = P(rows, cols)
    return jax.shard_map(
        per_device,
        mesh=fine,
        in_specs=(whole, whole, whole, whole, P(cols), whole),
        out_specs=whole,
        check_vma=False,
    )
```

time: 326 us -> 128 us (0.39)
  the two profiles are of different devices: /device:TPU:1 before, /device:TPU:22 now
where the time goes in v1:
time: 128 us; the launch traced here: 127 us
  blocking collectives  85.1 us (66%)
  local copies, waits for them, and re-layouts  13.5 us (11%)
  between operations  13.4 us (10%)
  waiting for transfers between devices  8.89 us (7%)
  Pallas kernels  4.2 us (3%)
  starting transfers between devices  1.91 us (1%)
    all_to_all x1, blocking collectives, per_device(): lax.all_to_all(packed, ('x', 'z'), split_axis=0, concat_axis=0, tiled=True)  38.8 us
    all_to_all x1, blocking collectives, per_device(): lax.all_to_all(conv, ('x', 'z'), split_axis=0, concat_axis=0, tiled=True)  21.5 us
    unnamed x26, local copies, waits for them, and re-layouts  13.5 us
    all_gather x1, blocking collectives, per_device(): near = lax.all_gather(out_weight, 'x', axis=0)  13.2 us
    all_gather x1, blocking collectives, per_device(): mine = lax.all_gather(gated, 'y', axis=0)  11.6 us
    all_gather x1, waiting for transfers between devices, per_device(): weight = lax.all_gather(near, 'z', axis=0)  8.87 us
  transfers between devices with their start and end apart: 2, of which 1 were waited for; matrix products, arithmetic and copies ran while one was open for 0% of the time, Pallas kernels for 2%

profile of v1, /device:TPU:22, one launch (start us, length us, event | category | flops | bytes accessed | tf_op | source)
XLA Modules:
  0.0 127.0 jit_solution(9792141776573193779)
XLA Ops:
  6.5 0.0 all-gather.5.cloned.1.call-start
  6.5 13.2 %all-gather = bf16[256,512]{1,0:T(8,128)(2,1)} all-gather(bf16[64,512]{1,0:T(8,128)(2,1)} %param.15), channel_id=2, replica_groups=mesh['x'=4,'z'=16,'y'=4,'core'=2] {'x'}, dimensions={0}, use_global_device_ids=true | all-gather | bytes 327680 | tf_op jit(solution)/shard_map/all_gather | solution.py:158
  19.7 0.9 copy-done.2
  20.6 0.0 copy-start.4
  20.6 0.9 copy-done.4
  21.5 0.9 copy-done.7
  22.4 0.1 shard_map.100
  22.6 0.0 all-gather.5.cloned.1.call-update
  22.6 38.8 %all_to_all.10.r_ref = bf16[64,16,128]{2,1,0:T(8,128)(2,1)S(1)} all-to-all(bf16[64,16,128]{2,1,0:T(8,128)(2,1)S(1)} %shard_map.100), channel_id=1, replica_groups=mesh['x'=4,'z'=16,'y'=4,'core'=2] {'x','z'}, dimensions={0} | all-to-all | bytes 524288 | tf_op jit(solution)/shard_map/all_to_all | solution.py:161
  61.5 0.0 copy-start.6
  61.5 1.0 copy-done.6
  62.5 0.0 copy-start.9
  62.5 0.8 copy-done.9
  63.3 0.0 copy-start.10
  63.3 0.8 copy-done.10
  64.1 0.0 copy-start.11
  64.1 0.8 copy-done.11
  64.9 2.4 %shard_map.101 = bf16[64,8,128]{2,1,0:T(8,128)(2,1)S(1)} custom-call(bf16[64,16,128]{2,1,0:T(8,128)(2,1)S(1)} %all_to_all.10.r_ref, bf16[128,128]{1,0:T(8,128)(2,1)S(1)} %copy-done.11, f32[2,64,128]{2,1,0:T(8,128)S(1)} %copy-done.9, bf16[4,256,256]{2,1,0:T(8,128)(2,1)S(1)} %copy-done.6, bf16[64,384]{1,0:T(8,128)(2,1)S(1)} %copy-done.10), custom_call_target="tpu_custom_call" | custom-call | tf_op jit(solution)/shard_map/pallas_call | solution.py:162
  67.3 21.5 %all_to_all.11.r_ref = bf16[64,8,128]{2,1,0:T(8,128)(2,1)S(1)} all-to-all(bf16[64,8,128]{2,1,0:T(8,128)(2,1)S(1)} %shard_map.101), channel_id=1, replica_groups=mesh['x'=4,'z'=16,'y'=4,'core'=2] {'x','z'}, dimensions={0} | all-to-all | bytes 262144 | tf_op jit(solution)/shard_map/all_to_all | solution.py:176
  88.8 0.9 copy-done.3
  89.7 0.9 copy-done.5
  90.6 0.9 copy-done.8
  91.5 0.7 copy-done.12
  92.2 0.1 shard_map.102
  92.3 11.6 %all-gather.1 = bf16[512,512]{1,0:T(8,128)(2,1)S(1)} all-gather(bf16[128,512]{1,0:T(8,128)(2,1)S(1)} %shard_map.102), channel_id=3, replica_groups=mesh['x'=4,'z'=16,'y'=4,'core'=2] {'y'}, dimensions={0}, use_global_device_ids=true | all-gather | bytes 655360 | tf_op jit(solution)/shard_map/all_gather | solution.py:180
  103.9 1.9 %collective-permute-start = (bf16[4,128,512]{2,1,0:T(8,128)(2,1)S(1)}, bf16[4,128,512]{2,1,0:T(8,128)(2,1)S(1)}, u32[]{:S(2)}, u32[]{:S(2)}) collective-permute-start(bf16[4,128,512]{2,1,0:T(8,128)(2,1)S(1)} %bitcast.7), channel_id=1, source_target_pairs={{0,1},{1,0},{2,3},{3,2},{4,5},{5,4},{6,7},{7,6},{8,9},{9,8},{10,11... | collective-permute-start | bytes 1572872 | tf_op jit(solution)/shard_map/ppermute | solution.py:181
  105.8 8.9 %all-gather.5.cloned.1.call-done = bf16[64,64,512]{2,1,0:T(8,128)(2,1)} async-done(((bf16[4,64,512]{2,1,0:T(8,128)(2,1)}), bf16[64,64,512]{2,1,0:T(8,128)(2,1)}) %all-gather.5.cloned.1.call-update) | async-done | bytes 4194320 | tf_op jit(solution)/shard_map/all_gather | solution.py:160
  114.7 2.2 %copy-done = bf16[64,64,512]{2,1,0:T(8,128)(2,1)S(1)} copy-done((bf16[64,64,512]{2,1,0:T(8,128)(2,1)S(1)}, bf16[64,64,512]{2,1,0:T(8,128)(2,1)}, u32[]{:S(2)}) %copy-start) | copy-done | bytes 4194328
  116.9 0.4 shard_map.103.p_ref
  117.3 0.0 collective-permute-done.g_ref
  117.3 1.7 %copy-done.1 = bf16[64,64,512]{2,1,0:T(8,128)(2,1)S(1)} copy-done((bf16[64,64,512]{2,1,0:T(8,128)(2,1)S(1)}, bf16[64,64,512]{2,1,0:T(8,128)(2,1)}, u32[]{:S(2)}) %copy-start.1) | copy-done | bytes 4194328
  119.1 1.1 shard_map.104
  (8 shorter events, 0.0 us)
Async XLA Ops:
  6.5 108.2 %all-gather.5.cloned.1.call-start = ((), (), s32[]{:S(2)}) async-start(), calls=%async_computation.2 | async-start | bytes 4456448 | tf_op jit(solution)/shard_map/all_gather | solution.py:160
  19.7 0.9 copy-start.2
  20.6 0.9 copy-start.4
  21.5 0.9 copy-start.7
  61.5 1.0 copy-start.6
  62.5 0.8 copy-start.9
  63.3 0.8 copy-start.10
  64.1 0.8 copy-start.11
  88.8 0.9 copy-start.3
  89.7 0.9 copy-start.5
  90.6 0.9 copy-start.8
  91.5 0.7 copy-start.12
  103.9 13.4 %collective-permute-start = (bf16[4,128,512]{2,1,0:T(8,128)(2,1)S(1)}, bf16[4,128,512]{2,1,0:T(8,128)(2,1)S(1)}, u32[]{:S(2)}, u32[]{:S(2)}) collective-permute-start(bf16[4,128,512]{2,1,0:T(8,128)(2,1)S(1)} %bitcast.7), channel_id=1, source_target_pairs={{0,1},{1,0},{2,3},{3,2},{4,5},{5,4},{6,7},{7,6},{8,9},{9,8},{10,11... | collective-permute-start | bytes 1572872 | tf_op jit(solution)/shard_map/ppermute | solution.py:181
  114.7 2.2 %copy-start = (bf16[64,64,512]{2,1,0:T(8,128)(2,1)S(1)}, bf16[64,64,512]{2,1,0:T(8,128)(2,1)}, u32[]{:S(2)}) copy-start(bf16[64,64,512]{2,1,0:T(8,128)(2,1)} %all-gather.5.cloned.1.call-done) | copy-start | bytes 12582916
  116.9 2.2 %copy-start.1 = (bf16[64,64,512]{2,1,0:T(8,128)(2,1)S(1)}, bf16[64,64,512]{2,1,0:T(8,128)(2,1)}, u32[]{:S(2)}) copy-start(bf16[64,64,512]{2,1,0:T(8,128)(2,1)} %all-gather.5.cloned.1.call-done) | copy-start | bytes 12582916
Sparse Core Ops, SparseCore 0:
  22.7 91.9 all-gather.4

commit v2 on v1

v2 whole, which is shorter than its diff:
```python
import math

import jax
import jax.numpy as jnp
import numpy as np
from jax import lax
from jax.experimental import pallas as pl
from jax.experimental.pallas import tpu as pltpu
from jax.sharding import Mesh
from jax.sharding import PartitionSpec as P

F32 = jnp.float32
BF16 = jnp.bfloat16
SEQ = 8192
BLOCK = 128
NBLK = SEQ // BLOCK
VMEM_LIMIT = 60 * 1024 * 1024


def tables():
    n1 = np.arange(NBLK)
    k1 = np.arange(NBLK) + 0.25
    n2 = np.arange(BLOCK)
    ang = 2.0 * math.pi / NBLK * (k1[:, None] * n1[None, :])
    first = np.concatenate([np.cos(ang), -np.sin(ang)], 0)
    first = np.concatenate([first, first], 1).astype(np.float32)
    tw = 2.0 * math.pi / SEQ * (k1[:, None] * n2[None, :])
    twist = np.stack([np.cos(tw), -np.sin(tw)]).astype(np.float32)
    th = 2.0 * math.pi / BLOCK * ((n2[:, None] * n2[None, :]) % BLOCK)
    c, s = np.cos(th), np.sin(th)
    fwd = np.block([[c, -s], [s, c]])
    second = np.stack([fwd, fwd.T]).astype(np.float32)
    last = (np.concatenate([np.cos(ang.T), -np.sin(ang.T)], 1) / SEQ).astype(np.float32)
    return first, twist, second, last


def split(x):
    high = x.astype(BF16)
    return high, (x - high.astype(F32)).astype(BF16)


def mm(a, b):
    return jnp.dot(a, b, preferred_element_type=F32)


def fetch(sources, buffers, sems):
    copies = [pltpu.make_async_copy(s, b, sems.at[i]) for i, (s, b) in enumerate(zip(sources, buffers))]
    for copy in copies:
        copy.start()
    return copies


def pack_kernel(gi_hbm, vi_hbm, f_hbm, out_ref, gi_ref, vi_ref, f_ref, sems):
    for copy in fetch((gi_hbm, vi_hbm, f_hbm), (gi_ref, vi_ref, f_ref), sems):
        copy.wait()
    signal = (gi_ref[...].astype(F32) * vi_ref[...].astype(F32)).astype(BF16)
    sig_t = signal.astype(F32).T.reshape(NBLK, 8, BLOCK)
    fil_t = f_ref[...].astype(F32).T.reshape(NBLK, 8, BLOCK)
    out_ref[...] = jnp.concatenate([sig_t, fil_t], 1).astype(BF16)


def conv_kernel(
    r_ref, first_hbm, twist_hbm, second_hbm, last_hbm, out_ref,
    xs, xx, hi, lo, spec, dd, ys, first_ref, twist_ref, second_ref, last_ref, sems,
):
    copies = fetch(
        (first_hbm, twist_hbm, second_hbm, last_hbm), (first_ref, twist_ref, second_ref, last_ref), sems
    )
    xs[...] = r_ref[...].astype(F32)
    for c in range(8):
        for part in range(2):
            x = xs[:, 8 * part + c, :].astype(BF16)
            at = pl.ds((2 * c + part) * BLOCK, BLOCK)
            xx[0:NBLK, at] = x
            xx[NBLK:, at] = x
    copies[0].wait()
    copies[1].wait()
    tre, tim = twist_ref[0], twist_ref[1]
    f_hi, f_lo = split(first_ref[...])
    lanes = lax.broadcasted_iota(jnp.int32, f_hi.shape, 1)
    first = jnp.where(lanes < NBLK, f_hi.astype(F32), f_lo.astype(F32)).astype(BF16)
    for j in range(16):
        a = mm(first, xx[:, j * BLOCK : (j + 1) * BLOCK])
        re, im = a[:NBLK], a[NBLK:]
        turned = jnp.concatenate([re * tre - im * tim, re * tim + im * tre], 1)
        rows = pl.ds(j * NBLK, NBLK)
        hi[rows, :], lo[rows, :] = split(turned)
    copies[2].wait()
    copies[3].wait()
    g_hi, g_lo = split(second_ref[0])
    spec[...] = mm(hi[...], g_hi) + mm(lo[...], g_hi) + mm(hi[...], g_lo)
    for c in range(8):
        s = spec[pl.ds(2 * c * NBLK, NBLK), :]
        f = spec[pl.ds((2 * c + 1) * NBLK, NBLK), :]
        sr, si, fr, fi = s[:, :BLOCK], s[:, BLOCK:], f[:, :BLOCK], f[:, BLOCK:]
        rows = pl.ds(c * NBLK, NBLK)
        hi[rows, :], lo[rows, :] = split(jnp.concatenate([sr * fr - si * fi, sr * fi + si * fr], 1))
    half = pl.ds(0, 8 * NBLK)
    g_hi, g_lo = split(second_ref[1])
    spec[half, :] = mm(hi[half, :], g_hi) + mm(lo[half, :], g_hi) + mm(hi[half, :], g_lo)
    for c in range(8):
        b = spec[pl.ds(c * NBLK, NBLK), :]
        br, bi = b[:, :BLOCK], b[:, BLOCK:]
        d_hi, d_lo = split(jnp.concatenate([br * tre + bi * tim, bi * tre - br * tim], 0))
        at = pl.ds(c * BLOCK, BLOCK)
        dd[0:128, at] = d_hi
        dd[128:256, at] = d_lo
        dd[256:384, at] = d_hi
    l_hi, l_lo = split(last_ref[...])
    y = mm(jnp.concatenate([l_hi, l_hi, l_lo], 1), dd[...])
    for c in range(8):
        ys[:, c, :] = y[:, c * BLOCK : (c + 1) * BLOCK]
    out_ref[...] = ys[...].astype(BF16)


def gate_kernel(r_ref, gi_hbm, vi_hbm, go_hbm, skip_ref, out_ref, gi_ref, vi_ref, go_ref, sems):
    copies = fetch((gi_hbm, vi_hbm, go_hbm), (gi_ref, vi_ref, go_ref), sems)
    conv = r_ref[...].astype(F32).reshape(8 * NBLK, BLOCK).T
    for copy in copies:
        copy.wait()
    signal = (gi_ref[...].astype(F32) * vi_ref[...].astype(F32)).astype(BF16).astype(F32)
    out_ref[...] = (go_ref[...].astype(F32) * (conv + skip_ref[...] * signal)).astype(BF16)


def project_kernel(mine_hbm, other_hbm, w_hbm, out_ref, g_ref, w_ref, g_sems, w_sems):
    core = lax.axis_index("core")
    g_copies = fetch((mine_hbm, other_hbm), (g_ref.at[0], g_ref.at[1]), g_sems)
    w_copies = []
    for side in range(2):
        start = 8 * (core if side == 0 else 1 - core)
        for y in range(4):
            at = 4 * side + y
            copy = pltpu.make_async_copy(w_hbm.at[pl.ds(start, 8), y], w_ref.at[at], w_sems.at[at])
            copy.start()
            w_copies.append(copy)
    total = jnp.zeros(out_ref.shape, F32)
    for at in range(8):
        if at % 4 == 0:
            g_copies[at // 4].wait()
        w_copies[at].wait()
        total += mm(g_ref[at // 4, at % 4], w_ref[at].reshape(512, 512))
    out_ref[...] = total.astype(BF16)


PARAMS = pltpu.CompilerParams(vmem_limit_bytes=VMEM_LIMIT)


def shape(dims, kind=BF16):
    return jax.ShapeDtypeStruct(dims, kind)


ANY = pl.BlockSpec(memory_space=pl.ANY)
INSIDE = pl.BlockSpec(memory_space=pltpu.VMEM)


def call(body, out, ins, scratch):
    return pl.pallas_call(
        body, out_shape=shape(out), in_specs=ins, out_specs=INSIDE, scratch_shapes=scratch, compiler_params=PARAMS
    )


def copies(count):
    return pltpu.SemaphoreType.DMA((count,))


def run_conv(moved):
    first, twist, second, last = tables()
    return call(
        conv_kernel,
        (NBLK, 8, BLOCK),
        [INSIDE, ANY, ANY, ANY, ANY],
        [
            pltpu.VMEM((NBLK, 16, BLOCK), F32),
            pltpu.VMEM((128, 16 * BLOCK), BF16),
            pltpu.VMEM((16 * NBLK, 256), BF16),
            pltpu.VMEM((16 * NBLK, 256), BF16),
            pltpu.VMEM((16 * NBLK, 256), F32),
            pltpu.VMEM((384, 8 * BLOCK), BF16),
            pltpu.VMEM((NBLK, 8, BLOCK), F32),
            pltpu.VMEM(first.shape, F32),
            pltpu.VMEM(twist.shape, F32),
            pltpu.VMEM(second.shape, F32),
            pltpu.VMEM(last.shape, F32),
            copies(4),
        ],
    )(moved, first, twist, second, last)


def per_device(gate_in, value_in, gate_out, filters, skip_gain, out_weight):
    tile = pltpu.VMEM((BLOCK, 512), BF16)
    near = lax.all_to_all(
        jnp.broadcast_to(out_weight[None], (4, 64, 512)), "x", split_axis=0, concat_axis=0, tiled=True
    )
    near, filters = lax.optimization_barrier((near, filters))
    weight = lax.all_gather(near, "z", axis=0)
    packed = call(pack_kernel, (NBLK, 16, BLOCK), [ANY] * 3, [tile] * 3 + [copies(3)])(gate_in, value_in, filters)
    moved = lax.all_to_all(packed, ("x", "z"), split_axis=0, concat_axis=0, tiled=True)
    conv = run_conv(moved)
    back = lax.all_to_all(conv, ("x", "z"), split_axis=0, concat_axis=0, tiled=True)
    gated = call(gate_kernel, (BLOCK, 512), [INSIDE, ANY, ANY, ANY, INSIDE], [tile] * 3 + [copies(3)])(
        back, gate_in, value_in, gate_out, skip_gain[None, :]
    )
    mine = lax.all_gather(gated, "y", axis=0)
    other = lax.ppermute(mine, "core", [(0, 1), (1, 0)])
    return call(
        project_kernel,
        (BLOCK, 512),
        [ANY] * 3,
        [
            pltpu.VMEM((2, 4, BLOCK, 512), BF16),
            pltpu.VMEM((8, 8, 64, 512), BF16),
            copies(2),
            copies(8),
        ],
    )(mine, other, weight)


def solution(mesh):
    fine = Mesh(mesh.devices.reshape(4, 16, 4, 2), ("x", "z", "y", "core"))
    rows, cols = ("x", "z"), ("y", "core")
    whole = P(rows, cols)
    return jax.shard_map(
        per_device,
        mesh=fine,
        in_specs=(whole, whole, whole, whole, P(cols), whole),
        out_specs=whole,
        check_vma=False,
    )
```

time: 128 us -> 123 us (0.961)
  the two profiles are of different devices: /device:TPU:22 before, /device:TPU:30 now
where the time goes in v2:
time: 123 us
  blocking collectives  86 us (70%)
  between operations  13.4 us (11%)
  Pallas kernels  12.9 us (10%)
  waiting for transfers between devices  7.42 us (6%)
  starting transfers between devices  1.91 us (2%)
    all_to_all x1, blocking collectives, per_device(): lax.all_to_all(packed, ('x', 'z'), split_axis=0, concat_axis=0, tiled=True)  41.1 us
    all_to_all x1, blocking collectives, per_device(): lax.all_to_all(conv, ('x', 'z'), split_axis=0, concat_axis=0, tiled=True)  22.1 us
    all_gather x1, blocking collectives, per_device(): mine = lax.all_gather(gated, 'y', axis=0)  13.5 us
    all_to_all x1, blocking collectives, per_device(): lax.all_to_all(jnp.broadcast_to(out_weight[None], (4, 64, 512)), 'x', spl...  9.29 us
    all_gather x1, waiting for transfers between devices, per_device(): weight = lax.all_gather(near, 'z', axis=0)  5.53 us
    pallas_call x1, Pallas kernels, run_conv(): call(conv_kernel, (NBLK, 8, BLOCK), [INSIDE, ANY, ANY, ANY, ANY], [pltpu....  4.55 us
    pallas_call x1, Pallas kernels, per_device(): call(project_kernel, (BLOCK, 512), [ANY] * 3, [pltpu.VMEM((2, 4, BLOCK, 5...  3.8 us
    pallas_call x1, Pallas kernels, per_device(): call(gate_kernel, (BLOCK, 512), [INSIDE, ANY, ANY, ANY, INSIDE], [tile] *...  2.7 us
  transfers between devices with their start and end apart: 2, of which 2 were waited for; matrix products, arithmetic and copies ran while one was open for 0% of the time, Pallas kernels for 7%

profile of v2, /device:TPU:30, one launch (start us, length us, event | category | flops | bytes accessed | tf_op | source)
XLA Modules:
  0.0 122.6 jit_solution(3893914722154843331)
XLA Ops:
  6.5 0.0 all-gather.4.cloned.1.call-start
  6.5 0.9 broadcast_in_dim.4
  7.4 9.3 %all_to_all.15 = bf16[4,64,512]{2,1,0:T(8,128)(2,1)} all-to-all(bf16[4,64,512]{2,1,0:T(8,128)(2,1)S(1)} %broadcast_in_dim.4), channel_id=1, replica_groups=mesh['x'=4,'z'=16,'y'=4,'core'=2] {'x'}, dimensions={0} | all-to-all | bytes 524288 | tf_op jit(solution)/shard_map/all_to_all | solution.py:191
  16.7 0.0 all-gather.4.cloned.1.call-update
  16.7 1.9 %shard_map.100 = bf16[64,16,128]{2,1,0:T(8,128)(2,1)} custom-call(bf16[128,512]{1,0:T(8,128)(2,1)} %gi_hbm.3, bf16[128,512]{1,0:T(8,128)(2,1)} %vi_hbm.3, bf16[128,512]{1,0:T(8,128)(2,1)} %f_hbm), custom_call_target="tpu_custom_call" | custom-call | tf_op jit(solution)/shard_map/pallas_call | solution.py:196
  18.6 41.1 %all_to_all.16.r_ref = bf16[64,16,128]{2,1,0:T(8,128)(2,1)} all-to-all(bf16[64,16,128]{2,1,0:T(8,128)(2,1)} %shard_map.100), channel_id=1, replica_groups=mesh['x'=4,'z'=16,'y'=4,'core'=2] {'x','z'}, dimensions={0} | all-to-all | bytes 524288 | tf_op jit(solution)/shard_map/all_to_all | solution.py:197
  59.7 4.6 %shard_map.101 = bf16[64,8,128]{2,1,0:T(8,128)(2,1)} custom-call(bf16[64,16,128]{2,1,0:T(8,128)(2,1)} %all_to_all.16.r_ref, f32[128,128]{1,0:T(8,128)} %constant.8.clone.first_hbm, f32[2,64,128]{2,1,0:T(8,128)} %constant.9.clone.twist_hbm, f32[2,256,256]{2,1,0:T(8,128)} %constant.10.clone.second_hbm, f32[64,128]{1,0:T(8,128)} %constant.11.clone.last_hbm), custom_call_target="tpu_custom_call" | custom-call | tf_op jit(solution)/shard_map/pallas_call | solution.py:168
  64.2 22.1 %all_to_all.17.r_ref = bf16[64,8,128]{2,1,0:T(8,128)(2,1)} all-to-all(bf16[64,8,128]{2,1,0:T(8,128)(2,1)} %shard_map.101), channel_id=1, replica_groups=mesh['x'=4,'z'=16,'y'=4,'core'=2] {'x','z'}, dimensions={0} | all-to-all | bytes 262144 | tf_op jit(solution)/shard_map/all_to_all | solution.py:199
  86.3 2.7 %shard_map.102 = bf16[128,512]{1,0:T(8,128)(2,1)} custom-call(bf16[64,8,128]{2,1,0:T(8,128)(2,1)} %all_to_all.17.r_ref, bf16[128,512]{1,0:T(8,128)(2,1)} %gi_hbm.3, bf16[128,512]{1,0:T(8,128)(2,1)} %vi_hbm.3, bf16[128,512]{1,0:T(8,128)(2,1)} %go_hbm.1, f32[1,512]{1,0:T(1,128)} %bitcast.6), custom_call_target="tpu_custom_call" | custom-call | tf_op jit(solution)/shard_map/pallas_call | solution.py:200
  89.1 13.5 %all-gather = bf16[512,512]{1,0:T(8,128)(2,1)S(1)} all-gather(bf16[128,512]{1,0:T(8,128)(2,1)} %shard_map.102), channel_id=2, replica_groups=mesh['x'=4,'z'=16,'y'=4,'core'=2] {'y'}, dimensions={0}, use_global_device_ids=true | all-gather | bytes 655360 | tf_op jit(solution)/shard_map/all_gather | solution.py:203
  102.6 0.0 copy-start
  102.6 1.9 %collective-permute-start = (bf16[4,128,512]{2,1,0:T(8,128)(2,1)S(1)}, bf16[4,128,512]{2,1,0:T(8,128)(2,1)S(1)}, u32[]{:S(2)}, u32[]{:S(2)}) collective-permute-start(bf16[4,128,512]{2,1,0:T(8,128)(2,1)S(1)} %bitcast.4), channel_id=1, source_target_pairs={{0,1},{1,0},{2,3},{3,2},{4,5},{5,4},{6,7},{7,6},{8,9},{9,8},{10,11... | collective-permute-start | bytes 1572872 | tf_op jit(solution)/shard_map/ppermute | solution.py:204
  104.5 1.9 %collective-permute-done.other_hbm = bf16[4,128,512]{2,1,0:T(8,128)(2,1)S(1)} collective-permute-done((bf16[4,128,512]{2,1,0:T(8,128)(2,1)S(1)}, bf16[4,128,512]{2,1,0:T(8,128)(2,1)S(1)}, u32[]{:S(2)}, u32[]{:S(2)}) %collective-permute-start) | collective-permute-done | bytes 524320 | tf_op jit(solution)/shard_map/ppermute | solution.py:204
  106.4 0.0 copy-start.1
  106.4 5.5 %all-gather.4.cloned.1.call-done = bf16[64,64,512]{2,1,0:T(8,128)(2,1)} async-done(((bf16[4,64,512]{2,1,0:T(8,128)(2,1)}), bf16[64,64,512]{2,1,0:T(8,128)(2,1)}) %all-gather.4.cloned.1.call-update) | async-done | bytes 4194320 | tf_op jit(solution)/shard_map/all_gather | solution.py:195
  111.9 0.0 copy-done
  111.9 0.0 copy-done.1
  111.9 3.8 %shard_map.103 = bf16[128,512]{1,0:T(8,128)(2,1)} custom-call(bf16[4,128,512]{2,1,0:T(8,128)(2,1)} %bitcast.5, bf16[4,128,512]{2,1,0:T(8,128)(2,1)} %copy-done.1, bf16[16,4,64,512]{3,2,1,0:T(8,128)(2,1)} %bitcast.3), custom_call_target="tpu_custom_call" | custom-call | tf_op jit(solution)/shard_map/pallas_call | solution.py:205
Async XLA Ops:
  6.5 105.4 %all-gather.4.cloned.1.call-start = ((), (), s32[]{:S(2)}) async-start(), calls=%async_computation.3 | async-start | bytes 4456448 | tf_op jit(solution)/shard_map/all_gather | solution.py:195
  102.6 9.3 %copy-start = (bf16[512,512]{1,0:T(8,128)(2,1)}, bf16[512,512]{1,0:T(8,128)(2,1)S(1)}, u32[]{:S(2)}) copy-start(bf16[512,512]{1,0:T(8,128)(2,1)S(1)} %all-gather) | copy-start | bytes 1572868
  102.6 3.8 %collective-permute-start = (bf16[4,128,512]{2,1,0:T(8,128)(2,1)S(1)}, bf16[4,128,512]{2,1,0:T(8,128)(2,1)S(1)}, u32[]{:S(2)}, u32[]{:S(2)}) collective-permute-start(bf16[4,128,512]{2,1,0:T(8,128)(2,1)S(1)} %bitcast.4), channel_id=1, source_target_pairs={{0,1},{1,0},{2,3},{3,2},{4,5},{5,4},{6,7},{7,6},{8,9},{9,8},{10,11... | collective-permute-start | bytes 1572872 | tf_op jit(solution)/shard_map/ppermute | solution.py:204
  106.4 5.5 %copy-start.1 = (bf16[4,128,512]{2,1,0:T(8,128)(2,1)}, bf16[4,128,512]{2,1,0:T(8,128)(2,1)S(1)}, u32[]{:S(2)}) copy-start(bf16[4,128,512]{2,1,0:T(8,128)(2,1)S(1)} %collective-permute-done.other_hbm) | copy-start | bytes 1572868
Sparse Core Ops, SparseCore 0:
  16.8 95.0 all-gather.3

commit v3 on v2

--- a/solution.py
+++ b/solution.py
@@ -14,7 +14,8 @@
 SEQ = 8192
 BLOCK = 128
 NBLK = SEQ // BLOCK
-VMEM_LIMIT = 60 * 1024 * 1024
+SPARE = 16
+VMEM_LIMIT = 24 * 1024 * 1024
 
 
 def tables():
@@ -50,17 +51,27 @@
     return copies
 
 
-def pack_kernel(gi_hbm, vi_hbm, f_hbm, out_ref, gi_ref, vi_ref, f_ref, sems):
-    for copy in fetch((gi_hbm, vi_hbm, f_hbm), (gi_ref, vi_ref, f_ref), sems):
-        copy.wait()
+def by_owner(x):
+    x = x.reshape(8, 4, 16, BLOCK)
+    return jnp.stack([x[:, owner] for owner in range(4)])
+
+
+def pack_kernel(gi_hbm, vi_hbm, f_hbm, go_hbm, w_hbm, out_ref, side_ref, gi_ref, vi_ref, f_ref, go_ref, w_ref, sems):
+    loads = fetch((go_hbm, w_hbm, gi_hbm, vi_hbm, f_hbm), (go_ref, w_ref, gi_ref, vi_ref, f_ref), sems)
+    for load in loads:
+        load.wait()
+    gate = by_owner(go_ref[...].astype(F32).T).reshape(4, BLOCK, BLOCK)
+    w = w_ref[...].astype(F32).reshape(4, 16, 512)
+    rows = [w[:, :, q * BLOCK : (q + 1) * BLOCK] for q in range(4)]
+    side_ref[...] = jnp.concatenate([gate] + rows, 1).astype(BF16)
     signal = (gi_ref[...].astype(F32) * vi_ref[...].astype(F32)).astype(BF16)
-    sig_t = signal.astype(F32).T.reshape(NBLK, 8, BLOCK)
-    fil_t = f_ref[...].astype(F32).T.reshape(NBLK, 8, BLOCK)
+    sig_t = by_owner(signal.astype(F32).T).reshape(NBLK, 8, BLOCK)
+    fil_t = by_owner(f_ref[...].astype(F32).T).reshape(NBLK, 8, BLOCK)
     out_ref[...] = jnp.concatenate([sig_t, fil_t], 1).astype(BF16)
 
 
 def conv_kernel(
-    r_ref, first_hbm, twist_hbm, second_hbm, last_hbm, out_ref,
+    r_ref, skip_ref, first_hbm, twist_hbm, second_hbm, last_hbm, out_ref,
     xs, xx, hi, lo, spec, dd, ys, first_ref, twist_ref, second_ref, last_ref, sems,
 ):
     copies = fetch(
@@ -108,38 +119,37 @@
         dd[256:384, at] = d_hi
     l_hi, l_lo = split(last_ref[...])
     y = mm(jnp.concatenate([l_hi, l_hi, l_lo], 1), dd[...])
-    for c in range(8):
-        ys[:, c, :] = y[:, c * BLOCK : (c + 1) * BLOCK]
-    out_ref[...] = ys[...].astype(BF16)
-
-
-def gate_kernel(r_ref, gi_hbm, vi_hbm, go_hbm, skip_ref, out_ref, gi_ref, vi_ref, go_ref, sems):
-    copies = fetch((gi_hbm, vi_hbm, go_hbm), (gi_ref, vi_ref, go_ref), sems)
-    conv = r_ref[...].astype(F32).reshape(8 * NBLK, BLOCK).T
-    for copy in copies:
-        copy.wait()
-    signal = (gi_ref[...].astype(F32) * vi_ref[...].astype(F32)).astype(BF16).astype(F32)
-    out_ref[...] = (go_ref[...].astype(F32) * (conv + skip_ref[...] * signal)).astype(BF16)
-
-
-def project_kernel(mine_hbm, other_hbm, w_hbm, out_ref, g_ref, w_ref, g_sems, w_sems):
+    at = lax.axis_index("z")
+    own = 64 * (at // 2) + 16 * lax.axis_index("x") + 8 * (at % 2)
+    for c in range(8):
+        direct = skip_ref[own + c] * xs[:, c, :]
+        ys[:, c, :] = y[:, c * BLOCK : (c + 1) * BLOCK] + direct
+    for x in range(4):
+        out_ref[:, x] = ys[pl.ds(16 * x, 16)].astype(BF16)
+
+
+def gate_kernel(r_ref, side_ref, out_ref):
+    for x in range(4):
+        conv = r_ref[:, x].astype(F32).reshape(BLOCK, BLOCK)
+        out_ref[x] = (conv * side_ref[x, 0:BLOCK].astype(F32)).T.astype(BF16)
+
+
+def project_kernel(mine_ref, other_ref, w_ref, out_ref):
     core = lax.axis_index("core")
-    g_copies = fetch((mine_hbm, other_hbm), (g_ref.at[0], g_ref.at[1]), g_sems)
-    w_copies = []
-    for side in range(2):
-        start = 8 * (core if side == 0 else 1 - core)
+    left, right = [], []
+    for side, ref in enumerate((mine_ref, other_ref)):
+        group = pl.ds(8 * (core if side == 0 else 1 - core), 8)
         for y in range(4):
-            at = 4 * side + y
-            copy = pltpu.make_async_copy(w_hbm.at[pl.ds(start, 8), y], w_ref.at[at], w_sems.at[at])
-            copy.start()
-            w_copies.append(copy)
-    total = jnp.zeros(out_ref.shape, F32)
-    for at in range(8):
-        if at % 4 == 0:
-            g_copies[at // 4].wait()
-        w_copies[at].wait()
-        total += mm(g_ref[at // 4, at % 4], w_ref[at].reshape(512, 512))
-    out_ref[...] = total.astype(BF16)
+            left.append(ref[y].reshape(4 * BLOCK, BLOCK))
+            w = w_ref[group, y, SPARE:].reshape(8, 4, 16, BLOCK)
+            right.append(jnp.concatenate([w[:, q].reshape(BLOCK, BLOCK) for q in range(4)], 1))
+    total = mm(jnp.concatenate(left, 1), jnp.concatenate(right, 0))
+    out_ref[...] = total.astype(BF16).reshape(4, BLOCK, 512)
+
+
+def sum_kernel(p_ref, out_ref):
+    p = p_ref[...].astype(F32)
+    out_ref[...] = ((p[0] + p[1]) + (p[2] + p[3])).astype(BF16)
 
 
 PARAMS = pltpu.CompilerParams(vmem_limit_bytes=VMEM_LIMIT)
@@ -150,6 +160,7 @@
 
 
 ANY = pl.BlockSpec(memory_space=pl.ANY)
+SCALARS = pl.BlockSpec(memory_space=pltpu.SMEM)
 INSIDE = pl.BlockSpec(memory_space=pltpu.VMEM)
 
 
@@ -163,12 +174,12 @@
     return pltpu.SemaphoreType.DMA((count,))
 
 
-def run_conv(moved):
+def run_conv(moved, skip):
     first, twist, second, last = tables()
     return call(
         conv_kernel,
-        (NBLK, 8, BLOCK),
-        [INSIDE, ANY, ANY, ANY, ANY],
+        (16, 4, 8, BLOCK),
+        [INSIDE, SCALARS, ANY, ANY, ANY, ANY],
         [
             pltpu.VMEM((NBLK, 16, BLOCK), F32),
             pltpu.VMEM((128, 16 * BLOCK), BF16),
@@ -183,36 +194,38 @@
             pltpu.VMEM(last.shape, F32),
             copies(4),
         ],
-    )(moved, first, twist, second, last)
+    )(moved, skip, first, twist, second, last)
 
 
 def per_device(gate_in, value_in, gate_out, filters, skip_gain, out_weight):
     tile = pltpu.VMEM((BLOCK, 512), BF16)
-    near = lax.all_to_all(
-        jnp.broadcast_to(out_weight[None], (4, 64, 512)), "x", split_axis=0, concat_axis=0, tiled=True
-    )
-    near, filters = lax.optimization_barrier((near, filters))
-    weight = lax.all_gather(near, "z", axis=0)
-    packed = call(pack_kernel, (NBLK, 16, BLOCK), [ANY] * 3, [tile] * 3 + [copies(3)])(gate_in, value_in, filters)
+    packed, side = pl.pallas_call(
+        pack_kernel,
+        out_shape=(shape((NBLK, 16, BLOCK)), shape((4, 192, BLOCK))),
+        in_specs=[ANY] * 5,
+        out_specs=(INSIDE, INSIDE),
+        scratch_shapes=[tile] * 4 + [pltpu.VMEM((64, 512), BF16), copies(5)],
+        compiler_params=pltpu.CompilerParams(vmem_limit_bytes=60 * 1024 * 1024),
+    )(gate_in, value_in, filters, gate_out, out_weight)
+    side = lax.all_to_all(side, "x", split_axis=0, concat_axis=0, tiled=True)
+    packed, side = lax.optimization_barrier((packed, side))
+    weight = lax.all_gather(side[:, BLOCK - SPARE :], "z", axis=0)
     moved = lax.all_to_all(packed, ("x", "z"), split_axis=0, concat_axis=0, tiled=True)
-    conv = run_conv(moved)
-    back = lax.all_to_all(conv, ("x", "z"), split_axis=0, concat_axis=0, tiled=True)
-    gated = call(gate_kernel, (BLOCK, 512), [INSIDE, ANY, ANY, ANY, INSIDE], [tile] * 3 + [copies(3)])(
-        back, gate_in, value_in, gate_out, skip_gain[None, :]
-    )
-    mine = lax.all_gather(gated, "y", axis=0)
+    conv = run_conv(moved, skip_gain)
+    back = lax.all_to_all(conv, "z", split_axis=0, concat_axis=0, tiled=True)
+    gated = call(gate_kernel, (4, BLOCK, BLOCK), [INSIDE, INSIDE], [])(back, side)
+    mine = lax.all_to_all(
+        jnp.broadcast_to(gated[None], (4, 4, BLOCK, BLOCK)), "y", split_axis=0, concat_axis=0, tiled=True
+    )
     other = lax.ppermute(mine, "core", [(0, 1), (1, 0)])
-    return call(
+    partial = call(
         project_kernel,
-        (BLOCK, 512),
-        [ANY] * 3,
-        [
-            pltpu.VMEM((2, 4, BLOCK, 512), BF16),
-            pltpu.VMEM((8, 8, 64, 512), BF16),
-            copies(2),
-            copies(8),
-        ],
+        (4, BLOCK, 512),
+        [INSIDE, INSIDE, INSIDE],
+        [],
     )(mine, other, weight)
+    parts = lax.all_to_all(partial, "x", split_axis=0, concat_axis=0, tiled=True)
+    return call(sum_kernel, (BLOCK, 512), [INSIDE], [])(parts)
 
 
 def solution(mesh):

time: 123 us -> 120 us (0.976)
  the two profiles are of different devices: /device:TPU:30 before, /device:TPU:16 now
where the time goes in v3:
time: 120 us
  blocking collectives  89.8 us (75%)
  between operations  13.5 us (11%)
  Pallas kernels  7.33 us (6%)
  waiting for transfers between devices  5.29 us (4%)
  local copies, waits for them, and re-layouts  2.07 us (2%)
  starting transfers between devices  1.95 us (2%)
    all_to_all x1, blocking collectives, per_device(): lax.all_to_all(packed, ('x', 'z'), split_axis=0, concat_axis=0, tiled=True)  38.8 us
    all_to_all x1, blocking collectives, per_device(): back = lax.all_to_all(conv, 'z', split_axis=0, concat_axis=0, tiled=True)  17.7 us
    all_to_all x1, blocking collectives, per_device(): lax.all_to_all(partial, 'x', split_axis=0, concat_axis=0, tiled=True)  12.6 us
    all_to_all x1, blocking collectives, per_device(): side = lax.all_to_all(side, 'x', split_axis=0, concat_axis=0, tiled=True)  10.6 us
    all_to_all x1, blocking collectives, per_device(): lax.all_to_all(jnp.broadcast_to(gated[None], (4, 4, BLOCK, BLOCK)), 'y',...  9.97 us
    pallas_call x1, Pallas kernels, run_conv(): call(conv_kernel, (16, 4, 8, BLOCK), [INSIDE, SCALARS, ANY, ANY, ANY, ANY...  3.69 us
    all_gather x1, waiting for transfers between devices, per_device(): weight = lax.all_gather(side[:, BLOCK - SPARE:], 'z', axis=0)  3.4 us
  transfers between devices with their start and end apart: 2, of which 2 were waited for; matrix products, arithmetic and copies ran while one was open for 0% of the time, Pallas kernels for 3%

profile of v3, /device:TPU:16, one launch (start us, length us, event | category | flops | bytes accessed | tf_op | source)
XLA Modules:
  0.0 119.9 jit_solution(11663168093358612101)
XLA Ops:
  6.5 0.0 copy-start.4
  6.5 0.0 copy-start.1
  6.5 0.0 copy-start.2
  6.5 0.0 copy-start.3
  6.5 0.0 copy-start.5
  6.5 0.0 all-gather.3.cloned.1.call-start
  6.6 2.1 %shard_map.100 = (bf16[64,16,128]{2,1,0:T(8,128)(2,1)}, bf16[4,192,128]{2,1,0:T(8,128)(2,1)}) custom-call(bf16[128,512]{1,0:T(8,128)(2,1)} %gi_hbm.1, bf16[128,512]{1,0:T(8,128)(2,1)} %vi_hbm.1, bf16[128,512]{1,0:T(8,128)(2,1)} %f_hbm.1, bf16[128,512]{1,0:T(8,128)(2,1)} %go_hbm.1, bf16[64,512]{1,0:T(8,128)(2,1)} %w_hbm.1), custom_call_target="tpu_custom_call" | custom-call | tf_op jit(solution)/shard_map/pallas_call | solution.py:202
  8.7 10.6 %all_to_all.25.side_ref = bf16[4,192,128]{2,1,0:T(8,128)(2,1)S(1)} all-to-all(bf16[4,192,128]{2,1,0:T(8,128)(2,1)} %get-tuple-element.10), channel_id=1, replica_groups=mesh['x'=4,'z'=16,'y'=4,'core'=2] {'x'}, dimensions={0} | all-to-all | bytes 393216 | tf_op jit(solution)/shard_map/all_to_all | solution.py:210
  19.3 0.6 slice.3
  20.0 0.0 all-gather.3.cloned.1.call-update
  20.0 38.8 %all_to_all.26.r_ref = bf16[64,16,128]{2,1,0:T(8,128)(2,1)S(1)} all-to-all(bf16[64,16,128]{2,1,0:T(8,128)(2,1)} %get-tuple-element.11), channel_id=1, replica_groups=mesh['x'=4,'z'=16,'y'=4,'core'=2] {'x','z'}, dimensions={0} | all-to-all | bytes 524288 | tf_op jit(solution)/shard_map/all_to_all | solution.py:213
  58.9 0.0 copy-done.4
  58.9 0.0 copy-done.1
  58.9 0.0 copy-done.2
  58.9 0.0 copy-done.3
  58.9 0.0 copy-done.5
  58.9 3.7 %shard_map.101 = bf16[16,4,8,128]{3,2,1,0:T(8,128)(2,1)S(1)} custom-call(bf16[64,16,128]{2,1,0:T(8,128)(2,1)S(1)} %all_to_all.26.r_ref, f32[512]{0:T(512)S(1)} %copy-done.5, f32[128,128]{1,0:T(8,128)S(1)} %copy-done.3, f32[2,64,128]{2,1,0:T(8,128)S(1)} %copy-done.2, f32[2,256,256]{2,1,0:T(8,128)S(1)} %copy-done.1, f32[64,128]{1,0:T(8,128)S(1)} %copy-done.4), custom_call_target="tpu_custom_call" | custom-call | tf_op jit(solution)/shard_map/pallas_call | solution.py:179
  62.6 17.7 %all_to_all.27.r_ref = bf16[16,4,8,128]{3,2,1,0:T(8,128)(2,1)S(1)} all-to-all(bf16[16,4,8,128]{3,2,1,0:T(8,128)(2,1)S(1)} %shard_map.101), channel_id=1, replica_groups=mesh['x'=4,'z'=16,'y'=4,'core'=2] {'z'}, dimensions={0} | all-to-all | bytes 262144 | tf_op jit(solution)/shard_map/all_to_all | solution.py:215
  80.3 0.1 shard_map.102
  80.4 0.1 broadcast_in_dim.2
  80.5 10.0 %all_to_all.28.mine_ref = bf16[4,4,128,128]{3,2,1,0:T(8,128)(2,1)S(1)} all-to-all(bf16[4,4,128,128]{3,2,1,0:T(8,128)(2,1)S(1)} %broadcast_in_dim.2), channel_id=1, replica_groups=mesh['x'=4,'z'=16,'y'=4,'core'=2] {'y'}, dimensions={0} | all-to-all | bytes 1048576 | tf_op jit(solution)/shard_map/all_to_all | solution.py:217
  90.5 1.9 %collective-permute-start = (bf16[4,4,128,128]{3,2,1,0:T(8,128)(2,1)S(1)}, bf16[4,4,128,128]{3,2,1,0:T(8,128)(2,1)S(1)}, u32[]{:S(2)}, u32[]{:S(2)}) collective-permute-start(bf16[4,4,128,128]{3,2,1,0:T(8,128)(2,1)S(1)} %all_to_all.28.mine_ref), channel_id=1, source_target_pairs={{0,1},{1,0},{2,3},{3,2},{4,5},{5,4},{6,7},{7,6},{8,9},{9,8},{10,11... | collective-permute-start | bytes 1572872 | tf_op jit(solution)/shard_map/ppermute | solution.py:220
  92.4 1.9 %collective-permute-done.other_ref = bf16[4,4,128,128]{3,2,1,0:T(8,128)(2,1)S(1)} collective-permute-done((bf16[4,4,128,128]{3,2,1,0:T(8,128)(2,1)S(1)}, bf16[4,4,128,128]{3,2,1,0:T(8,128)(2,1)S(1)}, u32[]{:S(2)}, u32[]{:S(2)}) %collective-permute-start) | collective-permute-done | bytes 524320 | tf_op jit(solution)/shard_map/ppermute | solution.py:220
  94.3 3.4 %all-gather.3.cloned.1.call-done = bf16[64,80,128]{2,1,0:T(8,128)(2,1)} async-done(((bf16[4,80,128]{2,1,0:T(8,128)(2,1)}), bf16[64,80,128]{2,1,0:T(8,128)(2,1)}) %all-gather.3.cloned.1.call-update) | async-done | bytes 1310736 | tf_op jit(solution)/shard_map/all_gather | solution.py:212
  97.7 0.0 copy-start
  97.7 1.3 %copy-done = bf16[64,80,128]{2,1,0:T(8,128)(2,1)S(1)} copy-done((bf16[64,80,128]{2,1,0:T(8,128)(2,1)S(1)}, bf16[64,80,128]{2,1,0:T(8,128)(2,1)}, u32[]{:S(2)}) %copy-start) | copy-done | bytes 1310744
  99.0 0.7 shard_map.103
  99.7 12.6 %all_to_all.29.p_ref = bf16[4,128,512]{2,1,0:T(8,128)(2,1)S(1)} all-to-all(bf16[4,128,512]{2,1,0:T(8,128)(2,1)S(1)} %shard_map.103), channel_id=1, replica_groups=mesh['x'=4,'z'=16,'y'=4,'core'=2] {'x'}, dimensions={0} | all-to-all | bytes 1048576 | tf_op jit(solution)/shard_map/all_to_all | solution.py:227
  112.3 0.7 shard_map.104
Async XLA Ops:
  6.5 52.3 %copy-start.4 = (f32[64,128]{1,0:T(8,128)S(1)}, f32[64,128]{1,0:T(8,128)}, u32[]{:S(2)}) copy-start(f32[64,128]{1,0:T(8,128)} %constant.11.clone.last_hbm) | copy-start | bytes 98308
  6.5 52.3 %copy-start.1 = (f32[2,256,256]{2,1,0:T(8,128)S(1)}, f32[2,256,256]{2,1,0:T(8,128)}, u32[]{:S(2)}) copy-start(f32[2,256,256]{2,1,0:T(8,128)} %constant.10.clone.second_hbm) | copy-start | bytes 1572868
  6.5 52.3 %copy-start.2 = (f32[2,64,128]{2,1,0:T(8,128)S(1)}, f32[2,64,128]{2,1,0:T(8,128)}, u32[]{:S(2)}) copy-start(f32[2,64,128]{2,1,0:T(8,128)} %constant.9.clone.twist_hbm) | copy-start | bytes 196612
  6.5 52.3 %copy-start.3 = (f32[128,128]{1,0:T(8,128)S(1)}, f32[128,128]{1,0:T(8,128)}, u32[]{:S(2)}) copy-start(f32[128,128]{1,0:T(8,128)} %constant.8.clone.first_hbm) | copy-start | bytes 196612
  6.5 52.3 %copy-start.5 = (f32[512]{0:T(512)S(1)}, f32[512]{0:T(512)}, u32[]{:S(2)}) copy-start(f32[512]{0:T(512)} %skip_ref.1) | copy-start | bytes 6148
  6.5 91.1 %all-gather.3.cloned.1.call-start = ((), (), s32[]{:S(2)}) async-start(), calls=%async_computation.5 | async-start | bytes 1392640 | tf_op jit(solution)/shard_map/all_gather | solution.py:212
  90.5 3.8 %collective-permute-start = (bf16[4,4,128,128]{3,2,1,0:T(8,128)(2,1)S(1)}, bf16[4,4,128,128]{3,2,1,0:T(8,128)(2,1)S(1)}, u32[]{:S(2)}, u32[]{:S(2)}) collective-permute-start(bf16[4,4,128,128]{3,2,1,0:T(8,128)(2,1)S(1)} %all_to_all.28.mine_ref), channel_id=1, source_target_pairs={{0,1},{1,0},{2,3},{3,2},{4,5},{5,4},{6,7},{7,6},{8,9},{9,8},{10,11... | collective-permute-start | bytes 1572872 | tf_op jit(solution)/shard_map/ppermute | solution.py:220
  97.7 1.3 %copy-start = (bf16[64,80,128]{2,1,0:T(8,128)(2,1)S(1)}, bf16[64,80,128]{2,1,0:T(8,128)(2,1)}, u32[]{:S(2)}) copy-start(bf16[64,80,128]{2,1,0:T(8,128)(2,1)} %all-gather.3.cloned.1.call-done) | copy-start | bytes 3932164
Sparse Core Ops, SparseCore 0:
  20.1 77.5 all-gather.2

commit v4 on v3

--- a/solution.py
+++ b/solution.py
@@ -71,12 +71,8 @@
 
 
 def conv_kernel(
-    r_ref, skip_ref, first_hbm, twist_hbm, second_hbm, last_hbm, out_ref,
-    xs, xx, hi, lo, spec, dd, ys, first_ref, twist_ref, second_ref, last_ref, sems,
+    r_ref, skip_ref, first_ref, twist_ref, second_ref, last_ref, out_ref, xs, xx, hi, lo, spec, dd, ys
 ):
-    copies = fetch(
-        (first_hbm, twist_hbm, second_hbm, last_hbm), (first_ref, twist_ref, second_ref, last_ref), sems
-    )
     xs[...] = r_ref[...].astype(F32)
     for c in range(8):
         for part in range(2):
@@ -84,8 +80,6 @@
             at = pl.ds((2 * c + part) * BLOCK, BLOCK)
             xx[0:NBLK, at] = x
             xx[NBLK:, at] = x
-    copies[0].wait()
-    copies[1].wait()
     tre, tim = twist_ref[0], twist_ref[1]
     f_hi, f_lo = split(first_ref[...])
     lanes = lax.broadcasted_iota(jnp.int32, f_hi.shape, 1)
@@ -96,8 +90,6 @@
         turned = jnp.concatenate([re * tre - im * tim, re * tim + im * tre], 1)
         rows = pl.ds(j * NBLK, NBLK)
         hi[rows, :], lo[rows, :] = split(turned)
-    copies[2].wait()
-    copies[3].wait()
     g_hi, g_lo = split(second_ref[0])
     spec[...] = mm(hi[...], g_hi) + mm(lo[...], g_hi) + mm(hi[...], g_lo)
     for c in range(8):
@@ -179,7 +171,7 @@
     return call(
         conv_kernel,
         (16, 4, 8, BLOCK),
-        [INSIDE, SCALARS, ANY, ANY, ANY, ANY],
+        [INSIDE, SCALARS, INSIDE, INSIDE, INSIDE, INSIDE],
         [
             pltpu.VMEM((NBLK, 16, BLOCK), F32),
             pltpu.VMEM((128, 16 * BLOCK), BF16),
@@ -188,11 +180,6 @@
             pltpu.VMEM((16 * NBLK, 256), F32),
             pltpu.VMEM((384, 8 * BLOCK), BF16),
             pltpu.VMEM((NBLK, 8, BLOCK), F32),
-            pltpu.VMEM(first.shape, F32),
-            pltpu.VMEM(twist.shape, F32),
-            pltpu.VMEM(second.shape, F32),
-            pltpu.VMEM(last.shape, F32),
-            copies(4),
         ],
     )(moved, skip, first, twist, second, last)
 

time: 120 us -> 120 us (level)
  the two profiles are of different devices: /device:TPU:16 before, /device:TPU:8 now
where the time goes in v4:
time: 120 us
  blocking collectives  91.6 us (76%)
  between operations  13.5 us (11%)
  Pallas kernels  6.79 us (6%)
  waiting for transfers between devices  4.01 us (3%)
  local copies, waits for them, and re-layouts  2.07 us (2%)
  starting transfers between devices  1.95 us (2%)
    all_to_all x1, blocking collectives, per_device(): lax.all_to_all(packed, ('x', 'z'), split_axis=0, concat_axis=0, tiled=True)  38.8 us
    all_to_all x1, blocking collectives, per_device(): back = lax.all_to_all(conv, 'z', split_axis=0, concat_axis=0, tiled=True)  17.6 us
    all_to_all x1, blocking collectives, per_device(): lax.all_to_all(partial, 'x', split_axis=0, concat_axis=0, tiled=True)  13 us
    all_to_all x1, blocking collectives, per_device(): lax.all_to_all(jnp.broadcast_to(gated[None], (4, 4, BLOCK, BLOCK)), 'y',...  11.6 us
    all_to_all x1, blocking collectives, per_device(): side = lax.all_to_all(side, 'x', split_axis=0, concat_axis=0, tiled=True)  10.6 us
    pallas_call x1, Pallas kernels, run_conv(): call(conv_kernel, (16, 4, 8, BLOCK), [INSIDE, SCALARS, INSIDE, INSIDE, IN...  3.15 us
  transfers between devices with their start and end apart: 2, of which 2 were waited for; matrix products, arithmetic and copies ran while one was open for 0% of the time, Pallas kernels for 3%

profile of v4, /device:TPU:8, one launch (start us, length us, event | category | flops | bytes accessed | tf_op | source)
XLA Modules:
  0.0 119.9 jit_solution(6323516937333833613)
XLA Ops:
  6.5 0.0 copy-start.4
  6.5 0.0 copy-start.1
  6.5 0.0 copy-start.2
  6.5 0.0 copy-start.3
  6.5 0.0 copy-start.5
  6.5 0.0 all-gather.3.cloned.1.call-start
  6.6 2.1 %shard_map.100 = (bf16[64,16,128]{2,1,0:T(8,128)(2,1)}, bf16[4,192,128]{2,1,0:T(8,128)(2,1)}) custom-call(bf16[128,512]{1,0:T(8,128)(2,1)} %gi_hbm.1, bf16[128,512]{1,0:T(8,128)(2,1)} %vi_hbm.1, bf16[128,512]{1,0:T(8,128)(2,1)} %f_hbm.1, bf16[128,512]{1,0:T(8,128)(2,1)} %go_hbm.1, bf16[64,512]{1,0:T(8,128)(2,1)} %w_hbm.1), custom_call_target="tpu_custom_call" | custom-call | tf_op jit(solution)/shard_map/pallas_call | solution.py:189
  8.7 10.6 %all_to_all.25.side_ref = bf16[4,192,128]{2,1,0:T(8,128)(2,1)S(1)} all-to-all(bf16[4,192,128]{2,1,0:T(8,128)(2,1)} %get-tuple-element.10), channel_id=1, replica_groups=mesh['x'=4,'z'=16,'y'=4,'core'=2] {'x'}, dimensions={0} | all-to-all | bytes 393216 | tf_op jit(solution)/shard_map/all_to_all | solution.py:197
  19.3 0.6 slice.3
  20.0 0.0 all-gather.3.cloned.1.call-update
  20.0 38.8 %all_to_all.26.r_ref = bf16[64,16,128]{2,1,0:T(8,128)(2,1)S(1)} all-to-all(bf16[64,16,128]{2,1,0:T(8,128)(2,1)} %get-tuple-element.11), channel_id=1, replica_groups=mesh['x'=4,'z'=16,'y'=4,'core'=2] {'x','z'}, dimensions={0} | all-to-all | bytes 524288 | tf_op jit(solution)/shard_map/all_to_all | solution.py:200
  58.8 0.0 copy-done.4
  58.8 0.0 copy-done.1
  58.8 0.0 copy-done.2
  58.8 0.0 copy-done.3
  58.8 0.0 copy-done.5
  58.8 3.2 %shard_map.101 = bf16[16,4,8,128]{3,2,1,0:T(8,128)(2,1)S(1)} custom-call(bf16[64,16,128]{2,1,0:T(8,128)(2,1)S(1)} %all_to_all.26.r_ref, f32[512]{0:T(512)S(1)} %copy-done.5, f32[128,128]{1,0:T(8,128)S(1)} %copy-done.3, f32[2,64,128]{2,1,0:T(8,128)S(1)} %copy-done.2, f32[2,256,256]{2,1,0:T(8,128)S(1)} %copy-done.1, f32[64,128]{1,0:T(8,128)S(1)} %copy-done.4), custom_call_target="tpu_custom_call" | custom-call | tf_op jit(solution)/shard_map/pallas_call | solution.py:171
  62.0 17.6 %all_to_all.27.r_ref = bf16[16,4,8,128]{3,2,1,0:T(8,128)(2,1)S(1)} all-to-all(bf16[16,4,8,128]{3,2,1,0:T(8,128)(2,1)S(1)} %shard_map.101), channel_id=1, replica_groups=mesh['x'=4,'z'=16,'y'=4,'core'=2] {'z'}, dimensions={0} | all-to-all | bytes 262144 | tf_op jit(solution)/shard_map/all_to_all | solution.py:202
  79.6 0.1 shard_map.102
  79.7 0.1 broadcast_in_dim.2
  79.8 11.6 %all_to_all.28.mine_ref = bf16[4,4,128,128]{3,2,1,0:T(8,128)(2,1)S(1)} all-to-all(bf16[4,4,128,128]{3,2,1,0:T(8,128)(2,1)S(1)} %broadcast_in_dim.2), channel_id=1, replica_groups=mesh['x'=4,'z'=16,'y'=4,'core'=2] {'y'}, dimensions={0} | all-to-all | bytes 1048576 | tf_op jit(solution)/shard_map/all_to_all | solution.py:204
  91.5 1.9 %collective-permute-start = (bf16[4,4,128,128]{3,2,1,0:T(8,128)(2,1)S(1)}, bf16[4,4,128,128]{3,2,1,0:T(8,128)(2,1)S(1)}, u32[]{:S(2)}, u32[]{:S(2)}) collective-permute-start(bf16[4,4,128,128]{3,2,1,0:T(8,128)(2,1)S(1)} %all_to_all.28.mine_ref), channel_id=1, source_target_pairs={{0,1},{1,0},{2,3},{3,2},{4,5},{5,4},{6,7},{7,6},{8,9},{9,8},{10,11... | collective-permute-start | bytes 1572872 | tf_op jit(solution)/shard_map/ppermute | solution.py:207
  93.4 1.9 %collective-permute-done.other_ref = bf16[4,4,128,128]{3,2,1,0:T(8,128)(2,1)S(1)} collective-permute-done((bf16[4,4,128,128]{3,2,1,0:T(8,128)(2,1)S(1)}, bf16[4,4,128,128]{3,2,1,0:T(8,128)(2,1)S(1)}, u32[]{:S(2)}, u32[]{:S(2)}) %collective-permute-start) | collective-permute-done | bytes 524320 | tf_op jit(solution)/shard_map/ppermute | solution.py:207
  95.3 2.1 %all-gather.3.cloned.1.call-done = bf16[64,80,128]{2,1,0:T(8,128)(2,1)} async-done(((bf16[4,80,128]{2,1,0:T(8,128)(2,1)}), bf16[64,80,128]{2,1,0:T(8,128)(2,1)}) %all-gather.3.cloned.1.call-update) | async-done | bytes 1310736 | tf_op jit(solution)/shard_map/all_gather | solution.py:199
  97.4 0.0 copy-start
  97.4 1.3 %copy-done = bf16[64,80,128]{2,1,0:T(8,128)(2,1)S(1)} copy-done((bf16[64,80,128]{2,1,0:T(8,128)(2,1)S(1)}, bf16[64,80,128]{2,1,0:T(8,128)(2,1)}, u32[]{:S(2)}) %copy-start) | copy-done | bytes 1310744
  98.7 0.7 shard_map.103
  99.4 13.0 %all_to_all.29.p_ref = bf16[4,128,512]{2,1,0:T(8,128)(2,1)S(1)} all-to-all(bf16[4,128,512]{2,1,0:T(8,128)(2,1)S(1)} %shard_map.103), channel_id=1, replica_groups=mesh['x'=4,'z'=16,'y'=4,'core'=2] {'x'}, dimensions={0} | all-to-all | bytes 1048576 | tf_op jit(solution)/shard_map/all_to_all | solution.py:214
  112.4 0.7 shard_map.104
Async XLA Ops:
  6.5 52.3 %copy-start.4 = (f32[64,128]{1,0:T(8,128)S(1)}, f32[64,128]{1,0:T(8,128)}, u32[]{:S(2)}) copy-start(f32[64,128]{1,0:T(8,128)} %constant.11.clone.last_ref) | copy-start | bytes 98308
  6.5 52.3 %copy-start.1 = (f32[2,256,256]{2,1,0:T(8,128)S(1)}, f32[2,256,256]{2,1,0:T(8,128)}, u32[]{:S(2)}) copy-start(f32[2,256,256]{2,1,0:T(8,128)} %constant.10.clone.second_ref) | copy-start | bytes 1572868
  6.5 52.3 %copy-start.2 = (f32[2,64,128]{2,1,0:T(8,128)S(1)}, f32[2,64,128]{2,1,0:T(8,128)}, u32[]{:S(2)}) copy-start(f32[2,64,128]{2,1,0:T(8,128)} %constant.9.clone.twist_ref) | copy-start | bytes 196612
  6.5 52.3 %copy-start.3 = (f32[128,128]{1,0:T(8,128)S(1)}, f32[128,128]{1,0:T(8,128)}, u32[]{:S(2)}) copy-start(f32[128,128]{1,0:T(8,128)} %constant.8.clone.first_ref) | copy-start | bytes 196612
  6.5 52.3 %copy-start.5 = (f32[512]{0:T(512)S(1)}, f32[512]{0:T(512)}, u32[]{:S(2)}) copy-start(f32[512]{0:T(512)} %skip_ref.1) | copy-start | bytes 6148
  6.5 90.8 %all-gather.3.cloned.1.call-start = ((), (), s32[]{:S(2)}) async-start(), calls=%async_computation.5 | async-start | bytes 1392640 | tf_op jit(solution)/shard_map/all_gather | solution.py:199
  91.5 3.8 %collective-permute-start = (bf16[4,4,128,128]{3,2,1,0:T(8,128)(2,1)S(1)}, bf16[4,4,128,128]{3,2,1,0:T(8,128)(2,1)S(1)}, u32[]{:S(2)}, u32[]{:S(2)}) collective-permute-start(bf16[4,4,128,128]{3,2,1,0:T(8,128)(2,1)S(1)} %all_to_all.28.mine_ref), channel_id=1, source_target_pairs={{0,1},{1,0},{2,3},{3,2},{4,5},{5,4},{6,7},{7,6},{8,9},{9,8},{10,11... | collective-permute-start | bytes 1572872 | tf_op jit(solution)/shard_map/ppermute | solution.py:207
  97.4 1.3 %copy-start = (bf16[64,80,128]{2,1,0:T(8,128)(2,1)S(1)}, bf16[64,80,128]{2,1,0:T(8,128)(2,1)}, u32[]{:S(2)}) copy-start(bf16[64,80,128]{2,1,0:T(8,128)(2,1)} %all-gather.3.cloned.1.call-done) | copy-start | bytes 3932164
Sparse Core Ops, SparseCore 0:
  20.1 77.1 all-gather.2

commit v5 on v4

--- a/solution.py
+++ b/solution.py
@@ -56,14 +56,19 @@
     return jnp.stack([x[:, owner] for owner in range(4)])
 
 
-def pack_kernel(gi_hbm, vi_hbm, f_hbm, go_hbm, w_hbm, out_ref, side_ref, gi_ref, vi_ref, f_ref, go_ref, w_ref, sems):
-    loads = fetch((go_hbm, w_hbm, gi_hbm, vi_hbm, f_hbm), (go_ref, w_ref, gi_ref, vi_ref, f_ref), sems)
+def side_kernel(go_hbm, w_hbm, side_ref, go_ref, w_ref, sems):
+    loads = fetch((go_hbm, w_hbm), (go_ref, w_ref), sems)
     for load in loads:
         load.wait()
     gate = by_owner(go_ref[...].astype(F32).T).reshape(4, BLOCK, BLOCK)
     w = w_ref[...].astype(F32).reshape(4, 16, 512)
     rows = [w[:, :, q * BLOCK : (q + 1) * BLOCK] for q in range(4)]
     side_ref[...] = jnp.concatenate([gate] + rows, 1).astype(BF16)
+
+
+def pack_kernel(gi_hbm, vi_hbm, f_hbm, out_ref, gi_ref, vi_ref, f_ref, sems):
+    for load in fetch((gi_hbm, vi_hbm, f_hbm), (gi_ref, vi_ref, f_ref), sems):
+        load.wait()
     signal = (gi_ref[...].astype(F32) * vi_ref[...].astype(F32)).astype(BF16)
     sig_t = by_owner(signal.astype(F32).T).reshape(NBLK, 8, BLOCK)
     fil_t = by_owner(f_ref[...].astype(F32).T).reshape(NBLK, 8, BLOCK)
@@ -186,16 +191,25 @@
 
 def per_device(gate_in, value_in, gate_out, filters, skip_gain, out_weight):
     tile = pltpu.VMEM((BLOCK, 512), BF16)
-    packed, side = pl.pallas_call(
+    wide = pltpu.CompilerParams(vmem_limit_bytes=60 * 1024 * 1024)
+    side = pl.pallas_call(
+        side_kernel,
+        out_shape=shape((4, 192, BLOCK)),
+        in_specs=[ANY] * 2,
+        out_specs=INSIDE,
+        scratch_shapes=[tile, pltpu.VMEM((64, 512), BF16), copies(2)],
+        compiler_params=wide,
+    )(gate_out, out_weight)
+    side = lax.all_to_all(side, "x", split_axis=0, concat_axis=0, tiled=True)
+    side, filters = lax.optimization_barrier((side, filters))
+    packed = pl.pallas_call(
         pack_kernel,
-        out_shape=(shape((NBLK, 16, BLOCK)), shape((4, 192, BLOCK))),
-        in_specs=[ANY] * 5,
-        out_specs=(INSIDE, INSIDE),
-        scratch_shapes=[tile] * 4 + [pltpu.VMEM((64, 512), BF16), copies(5)],
-        compiler_params=pltpu.CompilerParams(vmem_limit_bytes=60 * 1024 * 1024),
-    )(gate_in, value_in, filters, gate_out, out_weight)
-    side = lax.all_to_all(side, "x", split_axis=0, concat_axis=0, tiled=True)
-    packed, side = lax.optimization_barrier((packed, side))
+        out_shape=shape((NBLK, 16, BLOCK)),
+        in_specs=[ANY] * 3,
+        out_specs=INSIDE,
+        scratch_shapes=[tile] * 3 + [copies(3)],
+        compiler_params=wide,
+    )(gate_in, value_in, filters)
     weight = lax.all_gather(side[:, BLOCK - SPARE :], "z", axis=0)
     moved = lax.all_to_all(packed, ("x", "z"), split_axis=0, concat_axis=0, tiled=True)
     conv = run_conv(moved, skip_gain)

time: 120 us -> 121 us (level)
  Pallas kernels: 6.79 us -> 8.33 us
    pallas_call x1 -> x2, Pallas kernels: 2.11 us -> 3.65 us  [the longest x1 1.89 us: per_device(): pl.pallas_call(pack_kernel, out_shape=shape((NBLK, 16, BLOCK)), in_specs=...]
  transfers between devices with their start and end apart: 2 -> 2, of which waited for: 2 -> 2; matrix products, arithmetic and copies ran while one was open for 0% -> 0% of each run, Pallas kernels for 3% -> 4%
where the time goes in v5:
time: 121 us
  blocking collectives  92.2 us (76%)
  between operations  13.5 us (11%)
  Pallas kernels  8.33 us (7%)
  waiting for transfers between devices  2.85 us (2%)
  local copies, waits for them, and re-layouts  2.07 us (2%)
  starting transfers between devices  1.95 us (2%)
    all_to_all x1, blocking collectives, per_device(): lax.all_to_all(packed, ('x', 'z'), split_axis=0, concat_axis=0, tiled=True)  39.3 us
    all_to_all x1, blocking collectives, per_device(): back = lax.all_to_all(conv, 'z', split_axis=0, concat_axis=0, tiled=True)  17.7 us
    all_to_all x1, blocking collectives, per_device(): lax.all_to_all(partial, 'x', split_axis=0, concat_axis=0, tiled=True)  12.8 us
    all_to_all x1, blocking collectives, per_device(): lax.all_to_all(jnp.broadcast_to(gated[None], (4, 4, BLOCK, BLOCK)), 'y',...  11.8 us
    all_to_all x1, blocking collectives, per_device(): side = lax.all_to_all(side, 'x', split_axis=0, concat_axis=0, tiled=True)  10.6 us
    pallas_call x1, Pallas kernels, run_conv(): call(conv_kernel, (16, 4, 8, BLOCK), [INSIDE, SCALARS, INSIDE, INSIDE, IN...  3.15 us
  transfers between devices with their start and end apart: 2, of which 2 were waited for; matrix products, arithmetic and copies ran while one was open for 0% of the time, Pallas kernels for 4%

profile of v5, /device:TPU:8, one launch (start us, length us, event | category | flops | bytes accessed | tf_op | source)
XLA Modules:
  0.0 120.9 jit_solution(17000463656485310960)
XLA Ops:
  6.5 0.0 copy-start.4
  6.5 0.0 copy-start.1
  6.5 0.0 copy-start.2
  6.5 0.0 copy-start.3
  6.5 0.0 copy-start.5
  6.5 0.0 all-gather.3.cloned.1.call-start
  6.6 1.8 %shard_map.100 = bf16[4,192,128]{2,1,0:T(8,128)(2,1)} custom-call(bf16[128,512]{1,0:T(8,128)(2,1)} %go_hbm.1, bf16[64,512]{1,0:T(8,128)(2,1)} %w_hbm.1), custom_call_target="tpu_custom_call" | custom-call | tf_op jit(solution)/shard_map/pallas_call | solution.py:195
  8.4 10.6 %all_to_all.25.side_ref = bf16[4,192,128]{2,1,0:T(8,128)(2,1)S(1)} all-to-all(bf16[4,192,128]{2,1,0:T(8,128)(2,1)} %shard_map.100), channel_id=1, replica_groups=mesh['x'=4,'z'=16,'y'=4,'core'=2] {'x'}, dimensions={0} | all-to-all | bytes 393216 | tf_op jit(solution)/shard_map/all_to_all | solution.py:203
  19.0 0.6 slice.3
  19.6 0.0 all-gather.3.cloned.1.call-update
  19.7 1.9 %shard_map.101 = bf16[64,16,128]{2,1,0:T(8,128)(2,1)} custom-call(bf16[128,512]{1,0:T(8,128)(2,1)} %gi_hbm.1, bf16[128,512]{1,0:T(8,128)(2,1)} %vi_hbm.1, bf16[128,512]{1,0:T(8,128)(2,1)} %f_hbm), custom_call_target="tpu_custom_call" | custom-call | tf_op jit(solution)/shard_map/pallas_call | solution.py:205
  21.6 39.3 %all_to_all.26.r_ref = bf16[64,16,128]{2,1,0:T(8,128)(2,1)S(1)} all-to-all(bf16[64,16,128]{2,1,0:T(8,128)(2,1)} %shard_map.101), channel_id=1, replica_groups=mesh['x'=4,'z'=16,'y'=4,'core'=2] {'x','z'}, dimensions={0} | all-to-all | bytes 524288 | tf_op jit(solution)/shard_map/all_to_all | solution.py:214
  60.9 0.0 copy-done.4
  60.9 0.0 copy-done.1
  60.9 0.0 copy-done.2
  60.9 0.0 copy-done.3
  60.9 0.0 copy-done.5
  60.9 3.1 %shard_map.102 = bf16[16,4,8,128]{3,2,1,0:T(8,128)(2,1)S(1)} custom-call(bf16[64,16,128]{2,1,0:T(8,128)(2,1)S(1)} %all_to_all.26.r_ref, f32[512]{0:T(512)S(1)} %copy-done.5, f32[128,128]{1,0:T(8,128)S(1)} %copy-done.3, f32[2,64,128]{2,1,0:T(8,128)S(1)} %copy-done.2, f32[2,256,256]{2,1,0:T(8,128)S(1)} %copy-done.1, f32[64,128]{1,0:T(8,128)S(1)} %copy-done.4), custom_call_target="tpu_custom_call" | custom-call | tf_op jit(solution)/shard_map/pallas_call | solution.py:176
  64.1 17.7 %all_to_all.27.r_ref = bf16[16,4,8,128]{3,2,1,0:T(8,128)(2,1)S(1)} all-to-all(bf16[16,4,8,128]{3,2,1,0:T(8,128)(2,1)S(1)} %shard_map.102), channel_id=1, replica_groups=mesh['x'=4,'z'=16,'y'=4,'core'=2] {'z'}, dimensions={0} | all-to-all | bytes 262144 | tf_op jit(solution)/shard_map/all_to_all | solution.py:216
  81.7 0.1 shard_map.103
  81.8 0.1 broadcast_in_dim.2
  81.9 11.8 %all_to_all.28.mine_ref = bf16[4,4,128,128]{3,2,1,0:T(8,128)(2,1)S(1)} all-to-all(bf16[4,4,128,128]{3,2,1,0:T(8,128)(2,1)S(1)} %broadcast_in_dim.2), channel_id=1, replica_groups=mesh['x'=4,'z'=16,'y'=4,'core'=2] {'y'}, dimensions={0} | all-to-all | bytes 1048576 | tf_op jit(solution)/shard_map/all_to_all | solution.py:218
  93.7 1.9 %collective-permute-start = (bf16[4,4,128,128]{3,2,1,0:T(8,128)(2,1)S(1)}, bf16[4,4,128,128]{3,2,1,0:T(8,128)(2,1)S(1)}, u32[]{:S(2)}, u32[]{:S(2)}) collective-permute-start(bf16[4,4,128,128]{3,2,1,0:T(8,128)(2,1)S(1)} %all_to_all.28.mine_ref), channel_id=1, source_target_pairs={{0,1},{1,0},{2,3},{3,2},{4,5},{5,4},{6,7},{7,6},{8,9},{9,8},{10,11... | collective-permute-start | bytes 1572872 | tf_op jit(solution)/shard_map/ppermute | solution.py:221
  95.7 1.9 %collective-permute-done.other_ref = bf16[4,4,128,128]{3,2,1,0:T(8,128)(2,1)S(1)} collective-permute-done((bf16[4,4,128,128]{3,2,1,0:T(8,128)(2,1)S(1)}, bf16[4,4,128,128]{3,2,1,0:T(8,128)(2,1)S(1)}, u32[]{:S(2)}, u32[]{:S(2)}) %collective-permute-start) | collective-permute-done | bytes 524320 | tf_op jit(solution)/shard_map/ppermute | solution.py:221
  97.5 1.0 all-gather.3.cloned.1.call-done
  98.5 0.0 copy-start
  98.5 1.3 %copy-done = bf16[64,80,128]{2,1,0:T(8,128)(2,1)S(1)} copy-done((bf16[64,80,128]{2,1,0:T(8,128)(2,1)S(1)}, bf16[64,80,128]{2,1,0:T(8,128)(2,1)}, u32[]{:S(2)}) %copy-start) | copy-done | bytes 1310744
  99.8 0.7 shard_map.104
  100.5 12.8 %all_to_all.29.p_ref = bf16[4,128,512]{2,1,0:T(8,128)(2,1)S(1)} all-to-all(bf16[4,128,512]{2,1,0:T(8,128)(2,1)S(1)} %shard_map.104), channel_id=1, replica_groups=mesh['x'=4,'z'=16,'y'=4,'core'=2] {'x'}, dimensions={0} | all-to-all | bytes 1048576 | tf_op jit(solution)/shard_map/all_to_all | solution.py:228
  113.3 0.7 shard_map.105
Async XLA Ops:
  6.5 54.4 %copy-start.4 = (f32[64,128]{1,0:T(8,128)S(1)}, f32[64,128]{1,0:T(8,128)}, u32[]{:S(2)}) copy-start(f32[64,128]{1,0:T(8,128)} %constant.11.clone.last_ref) | copy-start | bytes 98308
  6.5 54.4 %copy-start.1 = (f32[2,256,256]{2,1,0:T(8,128)S(1)}, f32[2,256,256]{2,1,0:T(8,128)}, u32[]{:S(2)}) copy-start(f32[2,256,256]{2,1,0:T(8,128)} %constant.10.clone.second_ref) | copy-start | bytes 1572868
  6.5 54.4 %copy-start.2 = (f32[2,64,128]{2,1,0:T(8,128)S(1)}, f32[2,64,128]{2,1,0:T(8,128)}, u32[]{:S(2)}) copy-start(f32[2,64,128]{2,1,0:T(8,128)} %constant.9.clone.twist_ref) | copy-start | bytes 196612
  6.5 54.4 %copy-start.3 = (f32[128,128]{1,0:T(8,128)S(1)}, f32[128,128]{1,0:T(8,128)}, u32[]{:S(2)}) copy-start(f32[128,128]{1,0:T(8,128)} %constant.8.clone.first_ref) | copy-start | bytes 196612
  6.5 54.4 %copy-start.5 = (f32[512]{0:T(512)S(1)}, f32[512]{0:T(512)}, u32[]{:S(2)}) copy-start(f32[512]{0:T(512)} %skip_ref.1) | copy-start | bytes 6148
  6.5 91.9 %all-gather.3.cloned.1.call-start = ((), (), s32[]{:S(2)}) async-start(), calls=%async_computation.5 | async-start | bytes 1392640 | tf_op jit(solution)/shard_map/all_gather | solution.py:213
  93.7 3.8 %collective-permute-start = (bf16[4,4,128,128]{3,2,1,0:T(8,128)(2,1)S(1)}, bf16[4,4,128,128]{3,2,1,0:T(8,128)(2,1)S(1)}, u32[]{:S(2)}, u32[]{:S(2)}) collective-permute-start(bf16[4,4,128,128]{3,2,1,0:T(8,128)(2,1)S(1)} %all_to_all.28.mine_ref), channel_id=1, source_target_pairs={{0,1},{1,0},{2,3},{3,2},{4,5},{5,4},{6,7},{7,6},{8,9},{9,8},{10,11... | collective-permute-start | bytes 1572872 | tf_op jit(solution)/shard_map/ppermute | solution.py:221
  98.5 1.3 %copy-start = (bf16[64,80,128]{2,1,0:T(8,128)(2,1)S(1)}, bf16[64,80,128]{2,1,0:T(8,128)(2,1)}, u32[]{:S(2)}) copy-start(bf16[64,80,128]{2,1,0:T(8,128)(2,1)} %all-gather.3.cloned.1.call-done) | copy-start | bytes 3932164
Sparse Core Ops, SparseCore 0:
  19.8 78.6 all-gather.2
